TPU v7x, 32 devices: a whole 2x2x4 slice. The times are simulated.
32 devices in a mesh: section: 2 (over y), dp: 16 (over z, x, core).
Axes of the slice: x: 2, y: 2, z: 4, core: 2. Of those that a mesh axis runs over, the one named last changes fastest.
Arguments:
- queries: bfloat16 [4096, 3584], P(('section', 'dp')), may hold values from -1 to 1
- passages: bfloat16 [128, 16, 3584], P('dp'), may hold values from -1 to 1
- candidates: int32 [32, 3], P('section'), may hold values from 0 to 15, as said below
- counts: int32 [32], P('section'), may hold values from 1 to 3, 64 in all
- teacher: float32 [4096, 384], P(('section', 'dp')), may hold values from -20 to 450
- section_weights: bfloat16 [2, 3584, 3584], P('section', 'dp'), may hold values from -0.09375 to 0.09375
- section_inputs: bfloat16 [2, 16, 3584], P('section', None, 'dp'), may hold values from -1.5 to 1.5
- pre_acts: bfloat16 [2, 16, 3584], P('section', None, 'dp'), may hold values from -8 to 8
Outputs:
- query_grads: bfloat16 [4096, 3584], P(('section', 'dp'))
- passage_grads: bfloat16 [128, 16, 3584], P('dp')
- grad_inputs: float32 [2, 16, 3584], P('section', None, 'dp')
- weight_grads: bfloat16 [2, 3584, 3584], P('section', 'dp')
Inputs may be any that keep to these rules, and one draw needn't show every extreme that they name: `candidates`: each row names 3 different passage blocks. A query block uses the first counts[b] entries of its row of candidates.
All inputs are finite; a program needn't handle non-finite values.
Results may differ from a plain program's by a relative error of at most 0.0085.
Values may be sent and summed in bfloat16 or wider, within the bound.
A program may use at most 64 MiB of HBM per device.

v0:
```python
import jax
import jax.numpy as jnp
from jax import lax
from jax.sharding import PartitionSpec as P

INVERSE_TEMP = 20.0


def passed_along(value, axis, steps):
    count = lax.axis_size(axis)
    initial, last = (max(0, -steps), min(count, count - steps))
    return lax.ppermute(value, axis, [(source, source + steps) for source in range(initial, last)])


def soft_weights(logits, valid):
    masked = jnp.where(valid, logits, -1e30)
    highest = jnp.max(masked, axis=-1, keepdims=True)
    expons = jnp.where(valid, jnp.exp(masked - highest), 0.0)
    return expons / jnp.sum(expons, axis=-1, keepdims=True)


def body(queries, passages, candidates, counts, teacher, section_weights, section_inputs, pre_acts):
    dp_count = lax.axis_size("dp")
    dp_index = lax.axis_index("dp")
    stripe, block_total, width = passages.shape
    row_block_count = stripe * dp_count
    blocks_here = candidates.shape[0] // dp_count
    slot_count = candidates.shape[1]
    requests = blocks_here * slot_count
    all_slots = candidates.reshape(-1)
    outgoing = jnp.take(passages, all_slots, axis=1)
    pulled_rows = lax.all_to_all(outgoing, "dp", split_axis=1, concat_axis=0, tiled=True)
    pulled_rows = pulled_rows.reshape(row_block_count, blocks_here, slot_count, width)
    own_counts = lax.dynamic_slice_in_dim(counts, dp_index * blocks_here, blocks_here)
    slot_valid = jnp.arange(slot_count, dtype=jnp.int32)[None, :] < own_counts[:, None]
    column_valid = jnp.repeat(slot_valid, row_block_count, axis=1)[:, None, :]
    query_row_items = queries.reshape(blocks_here, row_block_count, width)
    logits = (
        jnp.einsum(
            "ixp,wifp->ixfw", query_row_items, pulled_rows, preferred_element_type=jnp.float32
        )
        * INVERSE_TEMP
    )
    logits = logits.reshape(blocks_here, row_block_count, slot_count * row_block_count)
    target_logits = soft_weights(
        teacher.reshape(blocks_here, row_block_count, slot_count * row_block_count), column_valid
    )
    weight_matrices = (soft_weights(logits, column_valid) - target_logits).astype(jnp.bfloat16)
    weight_matrices = weight_matrices.reshape(
        blocks_here, row_block_count, slot_count, row_block_count
    )
    query_sums = (
        jnp.einsum(
            "geal,lgay->gey", weight_matrices, pulled_rows, preferred_element_type=jnp.float32
        )
        * INVERSE_TEMP
    )
    passage_sums = (
        jnp.einsum(
            "fnyw,fnj->wfyj", weight_matrices, query_row_items, preferred_element_type=jnp.float32
        )
        * INVERSE_TEMP
    )
    block_terms = passage_sums.reshape(row_block_count, requests, width).astype(jnp.bfloat16)
    micro_count = section_inputs.shape[1] // dp_count
    col_width = width // dp_count
    micro_cols = jnp.transpose(
        query_sums[0, :micro_count].reshape(micro_count, dp_count, col_width), (1, 0, 2)
    )
    incoming_piece = lax.all_to_all(block_terms, "dp", split_axis=0, concat_axis=1, tiled=True)
    entry = lax.all_to_all(micro_cols, "dp", split_axis=0, concat_axis=1, tiled=True)
    onehot = (all_slots[:, None] == jnp.arange(block_total, dtype=jnp.int32)[None, :]).astype(
        jnp.float32
    )
    dense = jnp.einsum(
        "sjd,jn->snd",
        incoming_piece.astype(jnp.float32),
        onehot,
        precision=lax.Precision.HIGHEST,
        preferred_element_type=jnp.float32,
    )
    passage_out = lax.psum(dense, "section").astype(jnp.bfloat16)
    weight_rows = section_weights[0]
    input_cols = section_inputs[0]
    pre = pre_acts[0].astype(jnp.float32)
    sigma = jax.nn.sigmoid(pre)
    slope = sigma * (1.0 + pre * (1.0 - sigma))
    carry = entry.reshape(dp_count * micro_count, col_width)
    section_count = lax.axis_size("section")
    section_index = lax.axis_index("section")
    grad_cols = jnp.zeros_like(carry)
    grad_weight = jnp.zeros((col_width, width), jnp.float32)
    for section_turn in range(section_count):
        active_flag = section_count - 1 - section_turn
        inner = (carry * slope).astype(jnp.bfloat16)
        piece = lax.all_gather(inner, "dp", axis=1, tiled=True)
        back_sum = jnp.einsum("mj,ij->mi", piece, weight_rows, preferred_element_type=jnp.float32)
        weight_part = jnp.einsum("mi,mj->ij", input_cols, piece, preferred_element_type=jnp.float32)
        back_sum, layer_weight = (back_sum, weight_part)
        updated = carry + back_sum
        is_active = section_index == active_flag
        grad_cols = jnp.where(is_active, updated, grad_cols)
        grad_weight = jnp.where(is_active, layer_weight, grad_weight)
        if section_turn + 1 < section_count:
            carry = passed_along(updated, "section", -1)
    return (
        query_sums.reshape(blocks_here * row_block_count, width).astype(jnp.bfloat16),
        passage_out,
        grad_cols[None],
        grad_weight[None].astype(jnp.bfloat16),
    )


def solution(mesh):
    placed = (
        P(("section", "dp"), None),
        P("dp", None, None),
        P("section", None),
        P("section"),
        P(("section", "dp"), None),
        P("section", "dp", None),
        P("section", None, "dp"),
        P("section", None, "dp"),
    )
    return jax.shard_map(
        body,
        mesh=mesh,
        in_specs=placed,
        out_specs=(
            P(("section", "dp"), None),
            P("dp", None, None),
            P("section", None, "dp"),
            P("section", "dp", None),
        ),
        check_vma=False,
    )
```

profile of v0, /device:TPU:13, one launch (start us, length us, event | category | flops | bytes accessed | tf_op | source)
XLA Modules:
  0.0 280.4 jit_solution(6032910073845213975)
XLA Ops:
  0.6 0.9 copy.40
  1.7 12.4 %gather_fusion = bf16[48,8,3584]{2,0,1:T(8,128)(2,1)} fusion(bf16[8,16,3584]{2,1,0:T(8,128)(2,1)} %param.9, s32[1024]{0:T(1024)S(1)} %pad_clamp_fusion), kind=kCustom, calls=%fused_computation | custom fusion | bytes 5505216 | tf_op jit(solution)/shard_map/jit(_take)/gather | solution.py:31
  14.2 2.1 select_bitcast_fusion
  16.2 3.1 %copy.42 = bf16[8,48,3584]{2,0,1:T(8,128)(2,1)} copy(bf16[8,48,3584]{2,1,0:T(8,128)(2,1)S(1)} %select_bitcast_fusion) | data formatting | bytes 5505024 | tf_op jit(solution)/shard_map/jit(_take)/select_n | solution.py:31
  19.3 6.7 %all-to-all-start = ((bf16[8,48,3584]{2,0,1:T(8,128)(2,1)}), bf16[8,48,3584]{2,0,1:T(8,128)(2,1)}, u32[]{:S(2)}, u32[]{:S(2)}) async-start(bf16[8,48,3584]{2,0,1:T(8,128)(2,1)} %copy.42), calls=%async_computation | async-start | bytes 5505024 | tf_op jit(solution)/shard_map/all_to_all | solution.py:32
  26.2 0.6 dynamic_slice.3
  26.8 0.6 iota_compare_fusion.1
  27.6 0.1 fusion.44
  27.8 57.7 %all-to-all-done = bf16[8,48,3584]{2,0,1:T(8,128)(2,1)} async-done(((bf16[8,48,3584]{2,0,1:T(8,128)(2,1)}), bf16[8,48,3584]{2,0,1:T(8,128)(2,1)}, u32[]{:S(2)}, u32[]{:S(2)}) %all-to-all-start) | async-done | bytes 2752544 | tf_op jit(solution)/shard_map/all_to_all | solution.py:32
  85.4 2.7 fusion.42
  88.1 0.1 fusion.36
  88.3 0.2 fusion.43
  88.4 3.4 %fusion.60 = (bf16[128,3584]{1,0:T(8,128)(2,1)}, f32[128,3584]{1,0:T(8,128)S(1)}) fusion(bf16[128,3,128]{0,2,1:T(8,128)(2,1)S(1)} %bitcast.144, bf16[16,8,3,3584]{3,1,2,0:T(8,128)(2,1)} %bitcast.5), kind=kOutput, calls=%fused_computation.73 | convolution fusion | flops 353239040 | bytes 5603328 | tf_op jit(solution)/shard_map/geal,lgay->gey/dot_general | solution.py:53
  91.9 0.7 transpose_reshape_squeeze.4
  92.5 7.1 %all-to-all-start.2 = ((f32[16,1,224]{2,1,0:T(1,128)}), f32[16,1,224]{2,1,0:T(1,128)S(1)}, u32[]{:S(2)}, u32[]{:S(2)}) async-start(f32[16,1,224]{2,1,0:T(1,128)} %transpose_reshape_squeeze.4), calls=%async_computation.2 | async-start | bytes 32768 | tf_op jit(solution)/shard_map/all_to_all | solution.py:71
  99.6 0.9 fusion.2
  100.5 4.2 %copy.46 = bf16[128,3,3584]{2,1,0:T(4,128)(2,1)} copy(bf16[128,3,3584]{2,0,1:T(8,128)(2,1)S(1)} %fusion.2) | data formatting | bytes 5505024 | tf_op jit(solution)/shard_map/convert_element_type | solution.py:64
  104.7 6.2 %all-to-all-start.1 = ((bf16[128,3,3584]{2,1,0:T(4,128)(2,1)}), bf16[128,3,3584]{2,1,0:T(4,128)(2,1)}, u32[]{:S(2)}, u32[]{:S(2)}) async-start(bf16[128,3,3584]{2,1,0:T(4,128)(2,1)} %copy.46), calls=%async_computation.1 | async-start | bytes 7340032 | tf_op jit(solution)/shard_map/all_to_all | solution.py:70
  110.9 92.0 %all-gather = bf16[16,224,16]{1,2,0:T(8,128)(2,1)S(1)} all-gather(bf16[1,224,16]{1,2,0:T(8,128)(2,1)S(1)} %fusion.52), channel_id=1, replica_groups=mesh['section'=2,'dp'=16] {'dp'}, dimensions={0}, use_global_device_ids=true | all-gather | bytes 121856 | tf_op jit(solution)/shard_map/all_gather | solution.py:96
  202.9 0.2 reshape.254
  203.1 0.5 fusion.19
  203.6 2.4 collective-permute-start
  205.9 0.8 collective-permute-done
  206.8 17.8 %all-gather.1 = bf16[16,224,16]{1,2,0:T(8,128)(2,1)S(1)} all-gather(bf16[1,224,16]{1,2,0:T(8,128)(2,1)S(1)} %fusion.51), channel_id=1, replica_groups=mesh['section'=2,'dp'=16] {'dp'}, dimensions={0}, use_global_device_ids=true | all-gather | bytes 121856 | tf_op jit(solution)/shard_map/all_gather | solution.py:96
  224.7 0.2 reshape.256
  224.8 1.1 fusion.28
  226.0 0.6 fusion.54
  226.6 1.8 fusion.5
  228.4 2.6 copy.76
  231.0 0.2 copy.48
  231.2 1.6 convolution_bitcast_fusion
  232.8 47.6 %all-reduce.1 = bf16[8,16,3584]{2,1,0:T(8,128)(2,1)} all-reduce(f32[8,16,3584]{2,1,0:T(8,128)S(1)} %convolution_bitcast_fusion), channel_id=1, replica_groups=mesh['section'=2,'dp'=16] {'section'}, use_global_device_ids=true, to_apply=%region_4.5 | all-reduce | flops 458752 | bytes 2752512 | tf_op jit(solution)/shard_map/psum | solution.py:82
  (27 shorter events, 0.7 us)
Async XLA Ops:
  0.6 202.4 %copy-start = (bf16[1,224,3584]{2,1,0:T(8,128)(2,1)S(1)}, bf16[1,224,3584]{2,1,0:T(8,128)(2,1)}, u32[]{:S(2)}) copy-start(bf16[1,224,3584]{2,1,0:T(8,128)(2,1)} %param.13) | copy-start | bytes 4816900
  19.3 6.7 %copy-start.2 = (f32[128,384]{1,0:T(8,128)S(1)}, f32[128,384]{1,0:T(8,128)}, u32[]{:S(2)}) copy-start(f32[128,384]{1,0:T(8,128)} %param.12) | copy-start | bytes 589828
  19.3 6.9 %copy-start.5 = (s32[16]{0:T(128)S(1)}, s32[16]{0:T(128)}, u32[]{:S(2)}) copy-start(s32[16]{0:T(128)} %param.11) | copy-start | bytes 196
  19.3 66.1 %copy-start.1 = (bf16[128,3584]{1,0:T(8,128)(2,1)S(1)}, bf16[128,3584]{1,0:T(8,128)(2,1)}, u32[]{:S(2)}) copy-start(bf16[128,3584]{1,0:T(8,128)(2,1)} %param.8) | copy-start | bytes 2752516
  19.3 66.1 %all-to-all-start = ((bf16[8,48,3584]{2,0,1:T(8,128)(2,1)}), bf16[8,48,3584]{2,0,1:T(8,128)(2,1)}, u32[]{:S(2)}, u32[]{:S(2)}) async-start(bf16[8,48,3584]{2,0,1:T(8,128)(2,1)} %copy.42), calls=%async_computation | async-start | bytes 5505024 | tf_op jit(solution)/shard_map/all_to_all | solution.py:32
  92.5 12.1 %all-to-all-start.2 = ((f32[16,1,224]{2,1,0:T(1,128)}), f32[16,1,224]{2,1,0:T(1,128)S(1)}, u32[]{:S(2)}, u32[]{:S(2)}) async-start(f32[16,1,224]{2,1,0:T(1,128)} %transpose_reshape_squeeze.4), calls=%async_computation.2 | async-start | bytes 32768 | tf_op jit(solution)/shard_map/all_to_all | solution.py:71
  104.7 6.2 %copy-start.3 = (bf16[1,16,224]{2,1,0:T(8,128)(2,1)S(1)}, bf16[1,16,224]{2,1,0:T(8,128)(2,1)}, u32[]{:S(2)}) copy-start(bf16[1,16,224]{2,1,0:T(8,128)(2,1)} %param.15) | copy-start | bytes 21508
  104.7 123.7 %all-to-all-start.1 = ((bf16[128,3,3584]{2,1,0:T(4,128)(2,1)}), bf16[128,3,3584]{2,1,0:T(4,128)(2,1)}, u32[]{:S(2)}, u32[]{:S(2)}) async-start(bf16[128,3,3584]{2,1,0:T(4,128)(2,1)} %copy.46), calls=%async_computation.1 | async-start | bytes 7340032 | tf_op jit(solution)/shard_map/all_to_all | solution.py:70
  110.8 115.1 %copy-start.4 = (bf16[1,16,224]{2,1,0:T(8,128)(2,1)S(1)}, bf16[1,16,224]{2,1,0:T(8,128)(2,1)}, u32[]{:S(2)}) copy-start(bf16[1,16,224]{2,1,0:T(8,128)(2,1)} %param.14) | copy-start | bytes 21508
  203.6 3.2 %collective-permute-start = (f32[16,224]{1,0:T(8,128)S(1)}, f32[16,224]{1,0:T(8,128)S(1)}, u32[]{:S(2)}, u32[]{:S(2)}) collective-permute-start(f32[16,224]{1,0:T(8,128)S(1)} %fusion.19), channel_id=1, source_target_pairs={{16,0},{17,1},{18,2},{19,3},{20,4},{21,5},{22,6},{23,7},{24,8},{25... | collective-permute-start | bytes 43016 | tf_op jit(solution)/shard_map/ppermute | solution.py:12
where the time goes:
time: 286 us; the launch traced here: 280 us
  blocking collectives  157 us (55%)
  waiting for transfers between devices  58.5 us (20%)
  local copies, waits for them, and re-layouts  25.5 us (9%)
  starting transfers between devices  22.3 us (8%)
  matrix products  12.5 us (4%)
  other arithmetic  3.39 us (1%)
    all_gather x2, blocking collectives, body(): piece = lax.all_gather(inner, 'dp', axis=1, tiled=True)  110 us
    all_to_all x1, waiting for transfers between devices, body(): lax.all_to_all(outgoing, 'dp', split_axis=1, concat_axis=0, tiled=True)  57.7 us
    psum x1, blocking collectives, body(): passage_out = lax.psum(dense, 'section').astype(jnp.bfloat16)  47.6 us
    gather x1, local copies, waits for them, and re-layouts, body(): outgoing = jnp.take(passages, all_slots, axis=1)  12.4 us
    all_to_all x1, starting transfers between devices, body(): lax.all_to_all(micro_cols, 'dp', split_axis=0, concat_axis=1, tiled=True)  7.07 us
    all_to_all x1, starting transfers between devices, body(): lax.all_to_all(outgoing, 'dp', split_axis=1, concat_axis=0, tiled=True)  6.71 us
    all_to_all x1, starting transfers between devices, body(): lax.all_to_all(block_terms, 'dp', split_axis=0, concat_axis=1, tiled=True)  6.15 us
  transfers between devices with their start and end apart: 4, of which 2 were waited for; matrix products, arithmetic and copies ran while one was open for 4% of the time, Pallas kernels for 0%

commit v1 on v0

--- a/solution.py
+++ b/solution.py
@@ -1,6 +1,10 @@
+import functools
+
 import jax
 import jax.numpy as jnp
 from jax import lax
+from jax.experimental import pallas as pl
+from jax.experimental.pallas import tpu as pltpu
 from jax.sharding import PartitionSpec as P
 
 INVERSE_TEMP = 20.0
@@ -19,7 +23,7 @@
     return expons / jnp.sum(expons, axis=-1, keepdims=True)
 
 
-def body(queries, passages, candidates, counts, teacher, section_weights, section_inputs, pre_acts):
+def general_body(queries, passages, candidates, counts, teacher, section_weights, section_inputs, pre_acts):
     dp_count = lax.axis_size("dp")
     dp_index = lax.axis_index("dp")
     stripe, block_total, width = passages.shape
@@ -111,6 +115,480 @@
     )
 
 
+PLANE = 8
+GROUP = 4
+
+
+def cells(width, ref, index):
+    return ref.at[:, :, pl.ds(pl.multiple_of(index * width, width), width)]
+
+
+def relay_kernel(
+    q_ref, p_ref, cand_ref, teacher_ref, w_ref, inp_ref, pre_ref,
+    qg_ref, pg_ref, gi_ref, wg_ref,
+    candx, shard, up_in, down_in, sel, sel_t, stage, cols, target, terms, tin,
+    up_out, up_sum, down_out, down_sum, fin, final_in, prebuf, topbuf, cbuf, cot,
+    cand_s, cand_r, half_s, half_r, line_s, line_r, pull_s, pull_r, push_s, push_r,
+    sum_s, sum_r, fin_s, fin_r, pre_s, pre_r, top_s, top_r, cot_s, cot_r,
+):
+    dp_count = lax.axis_size("dp")
+    section = lax.axis_index("section")
+    dp = lax.axis_index("dp")
+    z = dp // GROUP
+    x = (dp // 2) % 2
+    core = dp % 2
+    me = x * 4 + section * 2 + core
+    quarter = section * 2 + core
+    z_count = dp_count // GROUP
+    stripe, block_total, width = p_ref.shape
+    part = width // 4
+    rows = 2 * stripe
+    block = q_ref.shape[0]
+    slots = teacher_ref.shape[1] // block
+    col = inp_ref.shape[1]
+    micro = inp_ref.shape[0]
+    f32, bf16 = jnp.float32, jnp.bfloat16
+
+    def remote(source, dest, send, recv, device):
+        return pltpu.make_async_remote_copy(
+            src_ref=source, dst_ref=dest, send_sem=send, recv_sem=recv,
+            device_id=device, device_id_type=pl.DeviceIdType.MESH,
+        )
+
+    def member(g):
+        return ((g // 2) % 2, z * GROUP + (g // 4) * 2 + g % 2)
+
+    def others(count, own, act):
+        def step(i, carry):
+            @pl.when(i != own)
+            def _():
+                act(i)
+            return carry
+        lax.fori_loop(0, count, step, 0)
+
+    barrier = pltpu.get_barrier_semaphore()
+    everyone = 2 * dp_count
+
+    def greet(i):
+        pl.semaphore_signal(
+            barrier, inc=1, device_id=(i // dp_count, i % dp_count),
+            device_id_type=pl.DeviceIdType.MESH,
+        )
+
+    others(everyone, section * dp_count + dp, greet)
+    pl.semaphore_wait(barrier, everyone - 1)
+
+    cand_copy = remote(cand_ref, candx, cand_s.at[0], cand_r.at[0], (1 - section, dp))
+    cand_copy.start()
+    partner = dp + 1 - 2 * core
+    half_copy = remote(
+        cells(part, p_ref, section * 2 + 1 - core), shard.at[pl.ds(core * stripe, stripe)],
+        half_s.at[0], half_r.at[0], (section, partner),
+    )
+    half_copy.start()
+    shard[pl.ds(core * stripe, stripe)] = p_ref[
+        :, :, pl.ds(pl.multiple_of(quarter * part, part), part)
+    ]
+    half_wait = remote(
+        cells(part, p_ref, quarter), shard.at[pl.ds((1 - core) * stripe, stripe)],
+        half_s.at[0], half_r.at[0], (section, partner),
+    )
+    half_wait.wait_recv()
+
+    def line_copy(source, ref, sems, h, step):
+        return remote(source, ref.at[h], line_s.at[sems, h], line_r.at[sems, h], (section, dp + step * GROUP))
+
+    @pl.when(z < z_count - 1)
+    def _():
+        line_copy(shard, up_in, 0, 0, 1).start()
+
+    @pl.when(z > 0)
+    def _():
+        line_copy(shard, down_in, 1, 0, -1).start()
+
+    cand_copy.wait_recv()
+    pieces = []
+    for g in range(PLANE):
+        at = z * GROUP + (g // 4) * 2 + g % 2
+        mine = cand_ref[pl.ds(at, 1), :]
+        away = candx[pl.ds(at, 1), :]
+        row = jnp.where(section == (g // 2) % 2, mine, away)
+        pieces.append(jnp.broadcast_to(row.astype(f32), (slots * rows, row.shape[1])))
+    listed = jnp.concatenate(pieces, axis=0)
+    total = PLANE * slots * rows
+    slot_of = (lax.broadcasted_iota(jnp.int32, listed.shape, 0) // rows) % slots
+    lane = lax.broadcasted_iota(jnp.int32, listed.shape, 1)
+    wanted = jnp.sum(jnp.where(lane == slot_of, listed, 0.0), axis=1, keepdims=True)
+    shape = (total, rows * block_total)
+    row_of = lax.broadcasted_iota(jnp.int32, shape, 0) % rows
+    place = lax.broadcasted_iota(jnp.int32, shape, 1)
+    hit = (place // block_total == row_of) & ((place % block_total).astype(f32) == wanted)
+    onehot = jnp.where(hit, 1.0, 0.0)
+    sel[...] = onehot.astype(bf16)
+    sel_t[...] = jnp.transpose(onehot).astype(bf16)
+
+    def own_rows(zs, at_x):
+        return pl.ds(pl.multiple_of(zs * GROUP * stripe + at_x * rows, rows), rows)
+
+    def pull_copy(zs, g):
+        return remote(
+            stage.at[zs, g], cols.at[quarter, :, own_rows(zs, x), :],
+            pull_s.at[zs, g], pull_r.at[zs, me], member(g),
+        )
+
+    def pull_wait(zs, g):
+        return remote(
+            stage.at[zs, g], cols.at[g % 4, :, own_rows(zs, g // 4), :],
+            pull_s.at[zs, g], pull_r.at[zs, g], member(g),
+        )
+
+    def spread(ref, zs):
+        picked = jnp.dot(
+            sel[...], ref[...].reshape(rows * block_total, part), preferred_element_type=f32
+        )
+        stage[zs] = picked.astype(bf16).reshape(PLANE, slots, rows, part)
+        others(PLANE, me, lambda g: pull_copy(zs, g).start())
+        cols[quarter, :, own_rows(zs, x), :] = stage[zs, me]
+
+    spread(shard, z)
+
+    prebuf[dp, :, :] = pre_ref[...]
+
+    def pre_copy(j):
+        return remote(prebuf.at[dp], prebuf.at[dp], pre_s.at[j], pre_r.at[dp], (section, j))
+
+    others(dp_count, dp, lambda j: pre_copy(j).start())
+
+    def soft(values, valid):
+        masked = jnp.where(valid, values, -1e30)
+        highest = jnp.max(masked, axis=-1, keepdims=True)
+        expons = jnp.where(valid, jnp.exp(masked - highest), 0.0)
+        return expons / jnp.sum(expons, axis=-1, keepdims=True)
+
+    own_row = cand_ref[pl.ds(dp, 1), :].astype(f32)
+    own_lane = lax.broadcasted_iota(jnp.int32, own_row.shape, 1)
+    how_many = jnp.sum(jnp.where(own_lane == slots, own_row, 0.0), axis=1, keepdims=True)
+    slot_lane = lax.broadcasted_iota(jnp.int32, teacher_ref.shape, 1) // block
+    valid = slot_lane.astype(f32) < how_many
+    target[...] = soft(teacher_ref[...], valid)
+
+    for h in range(z_count - 1):
+        @pl.when(z >= h + 1)
+        def _():
+            line_copy(shard, up_in, 0, h, -1).wait_recv()
+            if h + 1 < z_count - 1:
+                @pl.when(z < z_count - 1)
+                def _():
+                    line_copy(up_in.at[h], up_in, 0, h + 1, 1).start()
+
+        @pl.when(z + h + 1 < z_count)
+        def _():
+            line_copy(shard, down_in, 1, h, 1).wait_recv()
+            if h + 1 < z_count - 1:
+                @pl.when(z > 0)
+                def _():
+                    line_copy(down_in.at[h], down_in, 1, h + 1, -1).start()
+
+        @pl.when(z >= h + 1)
+        def _():
+            spread(up_in.at[h], z - h - 1)
+
+        @pl.when(z + h + 1 < z_count)
+        def _():
+            spread(down_in.at[h], z + h + 1)
+
+    for zs in range(z_count):
+        others(PLANE, me, lambda g: pull_wait(zs, g).wait_recv())
+
+    contract_last = (((1,), (1,)), ((), ()))
+    contract_first = (((0,), (0,)), ((), ()))
+    logits = jnp.zeros((block, slots * block), f32)
+    for f in range(4):
+        logits += lax.dot_general(
+            q_ref[:, f * part:(f + 1) * part], cols[f].reshape(slots * block, part),
+            contract_last, preferred_element_type=f32,
+        )
+    weights32 = soft(logits * INVERSE_TEMP, valid) - target[...]
+    weights = weights32.astype(bf16)
+    weights_t = jnp.transpose(weights32).astype(bf16)
+    for f in range(4):
+        sums = jnp.dot(weights, cols[f].reshape(slots * block, part), preferred_element_type=f32)
+        sums = sums * INVERSE_TEMP
+        qg_ref[:, f * part:(f + 1) * part] = sums.astype(bf16)
+        topbuf[dp, :, f * part:(f + 1) * part] = sums[0:1]
+
+    def top_copy(j):
+        return remote(topbuf.at[dp], topbuf.at[dp], top_s.at[j], top_r.at[dp], (section, j))
+
+    @pl.when(section == 1)
+    def _():
+        others(dp_count, dp, lambda j: top_copy(j).start())
+
+    for f in range(4):
+        sums = jnp.dot(
+            weights_t, q_ref[:, f * part:(f + 1) * part], preferred_element_type=f32
+        )
+        terms[f] = (sums * INVERSE_TEMP).astype(bf16).reshape(slots, block, part)
+
+    def push_copy(zt, g):
+        return remote(
+            terms.at[g % 4, :, own_rows(zt, g // 4), :], tin.at[zt, me],
+            push_s.at[zt, g], push_r.at[zt, me], member(g),
+        )
+
+    def push_wait(zt, g):
+        return remote(
+            terms.at[quarter, :, own_rows(zt, x), :], tin.at[zt, g],
+            push_s.at[zt, g], push_r.at[zt, g], member(g),
+        )
+
+    def push(zt):
+        others(PLANE, me, lambda g: push_copy(zt, g).start())
+        tin[zt, me] = terms[quarter, :, own_rows(zt, x), :]
+
+    for h in range(z_count - 1, 0, -1):
+        @pl.when(z + h < z_count)
+        def _():
+            push(z + h)
+
+        @pl.when(z >= h)
+        def _():
+            push(z - h)
+
+    push(z)
+
+    def cot_copy(j):
+        return remote(cbuf.at[dp], cbuf.at[dp], cot_s.at[j], cot_r.at[dp], (1 - section, j))
+
+    def layer(own):
+        others(dp_count, dp, lambda j: remote(
+            prebuf.at[j], prebuf.at[j], pre_s.at[j], pre_r.at[j], (section, j)).wait_recv())
+        pre = jnp.concatenate([prebuf[j].astype(f32)[:, :col] for j in range(dp_count)], axis=1)
+        sigma = 1.0 / (1.0 + jnp.exp(-pre))
+        slope = sigma * (1.0 + pre * (1.0 - sigma))
+        inner = (cot[...] * slope).astype(bf16)
+        back = lax.dot_general(inner, w_ref[...], contract_last, preferred_element_type=f32)
+        updated = own + back
+        gi_ref[...] = updated
+        inner_parts = [(f, inner[:, f * part:(f + 1) * part]) for f in range(4)]
+
+        def outer():
+            for f, piece in inner_parts:
+                wg_ref[:, f * part:(f + 1) * part] = lax.dot_general(
+                    inp_ref[...], piece, contract_first, preferred_element_type=f32
+                ).astype(bf16)
+
+        return updated, outer
+
+    @pl.when(section == 1)
+    def _():
+        others(dp_count, dp, lambda j: remote(
+            topbuf.at[j], topbuf.at[j], top_s.at[j], top_r.at[j], (section, j)).wait_recv())
+        own = jnp.zeros((micro, col), f32)
+        for j in range(dp_count):
+            cot[j:j + 1, :] = topbuf[j]
+        for j in range(dp_count):
+            own = jnp.where(dp == j, cot[:, j * col:(j + 1) * col], own)
+        updated, outer = layer(own)
+        cbuf[dp, :, :col] = updated
+        others(dp_count, dp_count, lambda j: cot_copy(j).start())
+        outer()
+
+    def summed(zt):
+        others(PLANE, me, lambda g: push_wait(zt, g).wait_recv())
+        return jnp.dot(
+            sel_t[...], tin[zt].reshape(total, part), preferred_element_type=f32
+        )
+
+    def sum_copy(source, dest, sems, h, step):
+        return remote(
+            source.at[h], dest.at[h], sum_s.at[sems, h], sum_r.at[sems, h],
+            (section, dp + step * GROUP),
+        )
+
+    def line_sum(h, zt, step, sems, out, incoming, beyond):
+        value = summed(zt)
+        fin_shape = (rows, block_total, part)
+        out[h - 1] = value.astype(bf16).reshape(fin_shape)
+        if h < z_count - 1:
+            @pl.when(beyond)
+            def _():
+                sum_copy(out, incoming, sems, h, -step).wait_recv()
+                out[h - 1] = (value.reshape(fin_shape) + incoming[h].astype(f32)).astype(bf16)
+        sum_copy(out, incoming, sems, h - 1, step).start()
+
+    for h in range(z_count - 1, 0, -1):
+        @pl.when(z + h < z_count)
+        def _():
+            line_sum(h, z + h, 1, 0, up_out, up_sum, z > 0)
+
+        @pl.when(z >= h)
+        def _():
+            line_sum(h, z - h, -1, 1, down_out, down_sum, z < z_count - 1)
+
+    value = summed(z).reshape(rows, block_total, part)
+
+    zero = jnp.zeros_like(value)
+    fin_acc = cot_like = None
+    @pl.when(z > 0)
+    def _():
+        sum_copy(up_out, up_sum, 0, 0, -1).wait_recv()
+
+    @pl.when(z < z_count - 1)
+    def _():
+        sum_copy(down_out, down_sum, 1, 0, 1).wait_recv()
+
+    below = jnp.where(z > 0, up_sum[0].astype(f32), zero)
+    above = jnp.where(z < z_count - 1, down_sum[0].astype(f32), zero)
+    fin[...] = (value + below + above).astype(bf16)
+
+    def fin_copy(i):
+        return remote(
+            fin.at[pl.ds((i % 2) * stripe, stripe)], final_in.at[quarter],
+            fin_s.at[i], fin_r.at[quarter], (i // 2, z * GROUP + x * 2 + i % 2),
+        )
+
+    def fin_wait(i):
+        return remote(
+            fin.at[pl.ds(core * stripe, stripe)], final_in.at[i],
+            fin_s.at[i], fin_r.at[i], (i // 2, z * GROUP + x * 2 + i % 2),
+        )
+
+    others(4, quarter, lambda i: fin_copy(i).start())
+    final_in[quarter] = fin[pl.ds(core * stripe, stripe)]
+
+    @pl.when(section == 0)
+    def _():
+        def wait(j, carry):
+            remote(cbuf.at[j], cbuf.at[j], cot_s.at[j], cot_r.at[j], (1 - section, j)).wait_recv()
+            return carry
+        lax.fori_loop(0, dp_count, wait, 0)
+        cot[...] = jnp.concatenate([cbuf[j][:, :col] for j in range(dp_count)], axis=1)
+        updated, outer = layer(cbuf[dp][:, :col])
+        outer()
+
+    others(4, quarter, lambda i: fin_wait(i).wait_recv())
+    for f in range(4):
+        pg_ref[:, :, f * part:(f + 1) * part] = final_in[f]
+
+    cand_copy.wait_send()
+    half_copy.wait_send()
+    for h in range(z_count - 1):
+        @pl.when((z >= h) & (z < z_count - 1))
+        def _():
+            line_copy(up_in.at[h], up_in, 0, h, 1).wait_send()
+
+        @pl.when((z + h < z_count) & (z > 0))
+        def _():
+            line_copy(down_in.at[h], down_in, 1, h, -1).wait_send()
+
+        @pl.when(z + h + 1 < z_count)
+        def _():
+            sum_copy(up_out, up_sum, 0, h, 1).wait_send()
+
+        @pl.when(z >= h + 1)
+        def _():
+            sum_copy(down_out, down_sum, 1, h, -1).wait_send()
+
+    for zs in range(z_count):
+        others(PLANE, me, lambda g: pull_copy(zs, g).wait_send())
+        others(PLANE, me, lambda g: push_copy(zs, g).wait_send())
+    others(dp_count, dp, lambda j: pre_copy(j).wait_send())
+
+    @pl.when(section == 1)
+    def _():
+        others(dp_count, dp, lambda j: top_copy(j).wait_send())
+        others(dp_count, dp_count, lambda j: cot_copy(j).wait_send())
+
+    others(4, quarter, lambda i: fin_copy(i).wait_send())
+
+
+def plane_body(queries, passages, candidates, counts, teacher, section_weights, section_inputs, pre_acts):
+    dp_count = lax.axis_size("dp")
+    z_count = dp_count // GROUP
+    stripe, block_total, width = passages.shape
+    block = queries.shape[0]
+    slots = candidates.shape[1]
+    part = width // 4
+    rows = 2 * stripe
+    micro, col = section_inputs.shape[1:]
+    wide = -(-col // 128) * 128
+    f32, bf16, i32 = jnp.float32, jnp.bfloat16, jnp.int32
+    table = jnp.concatenate([candidates, counts[:, None]], axis=1)
+    table = jnp.pad(table, ((0, 0), (0, 128 - slots - 1)))
+    pre = jnp.pad(pre_acts[0], ((0, 0), (0, wide - col)))
+    vmem, dma = pltpu.VMEM, pltpu.SemaphoreType.DMA
+    hop = z_count - 1
+    scratch = [
+        vmem(table.shape, i32),
+        vmem((rows, block_total, part), bf16),
+        vmem((hop, rows, block_total, part), bf16),
+        vmem((hop, rows, block_total, part), bf16),
+        vmem((PLANE * slots * rows, rows * block_total), bf16),
+        vmem((rows * block_total, PLANE * slots * rows), bf16),
+        vmem((z_count, PLANE, slots, rows, part), bf16),
+        vmem((4, slots, block, part), bf16),
+        vmem((block, slots * block), f32),
+        vmem((4, slots, block, part), bf16),
+        vmem((z_count, PLANE, slots, rows, part), bf16),
+        vmem((hop, rows, block_total, part), bf16),
+        vmem((hop, rows, block_total, part), bf16),
+        vmem((hop, rows, block_total, part), bf16),
+        vmem((hop, rows, block_total, part), bf16),
+        vmem((rows, block_total, part), bf16),
+        vmem((4, stripe, block_total, part), bf16),
+        vmem((dp_count, micro, wide), bf16),
+        vmem((dp_count, 1, width), f32),
+        vmem((dp_count, micro, wide), f32),
+        vmem((micro, width), f32),
+        dma((1,)), dma((1,)), dma((1,)), dma((1,)),
+        dma((2, hop)), dma((2, hop)),
+        dma((z_count, PLANE)), dma((z_count, PLANE)),
+        dma((z_count, PLANE)), dma((z_count, PLANE)),
+        dma((2, hop)), dma((2, hop)),
+        dma((4,)), dma((4,)),
+        dma((dp_count,)), dma((dp_count,)),
+        dma((dp_count,)), dma((dp_count,)),
+        dma((dp_count,)), dma((dp_count,)),
+    ]
+    here = pl.BlockSpec(memory_space=vmem)
+    query_grads, passage_grads, grad_inputs, weight_grads = pl.pallas_call(
+        relay_kernel,
+        out_shape=(
+            jax.ShapeDtypeStruct(queries.shape, bf16),
+            jax.ShapeDtypeStruct(passages.shape, bf16),
+            jax.ShapeDtypeStruct((micro, col), f32),
+            jax.ShapeDtypeStruct(section_weights.shape[1:], bf16),
+        ),
+        in_specs=[here] * 7,
+        out_specs=(here,) * 4,
+        scratch_shapes=scratch,
+        compiler_params=pltpu.CompilerParams(
+            collective_id=0, has_side_effects=True, vmem_limit_bytes=56 * 1024 * 1024
+        ),
+    )(queries, passages, table, teacher, section_weights[0], section_inputs[0], pre)
+    return query_grads, passage_grads, grad_inputs[None], weight_grads[None]
+
+
+def body(queries, passages, candidates, counts, teacher, section_weights, section_inputs, pre_acts):
+    sections, dp_count = lax.axis_size("section"), lax.axis_size("dp")
+    stripe, block_total, width = passages.shape
+    by_planes = (
+        sections == 2
+        and dp_count == 16
+        and stripe == 8
+        and block_total == 16
+        and width % 512 == 0
+        and candidates.shape[0] == dp_count
+        and candidates.shape[1] * dp_count * stripe == teacher.shape[1]
+        and section_inputs.shape[1] == dp_count
+    )
+    chosen = plane_body if by_planes else general_body
+    return chosen(
+        queries, passages, candidates, counts, teacher, section_weights, section_inputs, pre_acts
+    )
+
+
 def solution(mesh):
     placed = (
         P(("section", "dp"), None),

time: 286 us -> 130 us (0.45)
  the two profiles are of different devices: /device:TPU:13 before, /device:TPU:1 now
where the time goes in v1:
time: 130 us
  Pallas kernels  121 us (93%)
  local copies, waits for them, and re-layouts  7 us (5%)
    pallas_call x1, Pallas kernels, plane_body(): pl.pallas_call(relay_kernel, out_shape=(jax.ShapeDtypeStruct(queries.shap...  121 us
    unnamed x10, local copies, waits for them, and re-layouts  5 us

profile of v1, /device:TPU:1, one launch (start us, length us, event | category | flops | bytes accessed | tf_op | source)
XLA Modules:
  0.0 129.8 jit_solution(17832251565813491441)
XLA Ops:
  0.6 0.7 pad_add_fusion
  1.3 0.1 copy.14
  1.4 0.6 pad.8.cand_ref
  2.0 1.3 %pad.9.pre_ref = bf16[16,256]{1,0:T(8,128)(2,1)} pad(bf16[16,224]{1,0:T(8,128)(2,1)} %bitcast.10, bf16[]{:T(256)} %constant.3.clone.1), padding=0_0x0_32 | pad | bytes 15362 | tf_op jit(solution)/shard_map/jit(_pad)/pad | solution.py:519
  3.3 121.4 %shard_map.111 = (bf16[128,3584]{1,0:T(8,128)(2,1)}, bf16[8,16,3584]{2,1,0:T(8,128)(2,1)}, f32[16,224]{1,0:T(8,128)}, bf16[224,3584]{1,0:T(8,128)(2,1)}) custom-call(bf16[128,3584]{1,0:T(8,128)(2,1)} %q_ref.1, bf16[8,16,3584]{2,1,0:T(8,128)(2,1)} %p_ref.1, s32[16,128]{1,0:T(8,128)} %pad.8.cand_ref, f32[128,384]{1,0:T(8,128)} %teacher_ref.1, ...), custom_call_target="tpu_custom_call" | custom-call | tf_op jit(solution)/shard_map/pallas_call | solution.py:555
  124.7 0.0 copy-start.1
  124.8 0.0 copy-start.2
  124.8 0.0 copy-start
  124.8 2.3 %copy.19 = bf16[128,3584]{1,0:T(8,128)(2,1)} copy(bf16[128,3584]{1,0:T(8,128)(2,1)} %get-tuple-element.16) | data formatting | bytes 1835008
  127.1 0.0 copy-done.1
  127.1 0.9 copy.20
  128.0 0.0 copy-done.2
  128.0 0.6 copy.21
  128.6 0.0 copy-done
  128.6 1.2 copy.22
Async XLA Ops:
  124.7 2.3 %copy-start.1 = (bf16[8,16,3584]{2,1,0:T(8,128)(2,1)S(1)}, bf16[8,16,3584]{2,1,0:T(8,128)(2,1)}, u32[]{:S(2)}) copy-start(bf16[8,16,3584]{2,1,0:T(8,128)(2,1)} %get-tuple-element.17) | copy-start | bytes 2752516
  124.8 3.3 %copy-start.2 = (f32[16,224]{1,0:T(8,128)S(1)}, f32[16,224]{1,0:T(8,128)}, u32[]{:S(2)}) copy-start(f32[16,224]{1,0:T(8,128)} %get-tuple-element.10) | copy-start | bytes 43012
  124.8 3.9 %copy-start = (bf16[224,3584]{1,0:T(8,128)(2,1)S(1)}, bf16[224,3584]{1,0:T(8,128)(2,1)}, u32[]{:S(2)}) copy-start(bf16[224,3584]{1,0:T(8,128)(2,1)} %get-tuple-element.11) | copy-start | bytes 4816900

commit v2 on v1

--- a/solution.py
+++ b/solution.py
@@ -124,8 +124,9 @@
 
 
 def relay_kernel(
-    q_ref, p_ref, cand_ref, teacher_ref, w_ref, inp_ref, pre_ref,
-    qg_ref, pg_ref, gi_ref, wg_ref,
+    q_hbm, p_ref, cand_ref, count_ref, teacher_hbm, w_hbm, pre_ref,
+    qg_hbm, pg_ref, gi_ref, inner_ref,
+    q_ref, teacher_ref, w_ref, qg_ref, load_s, store_s,
     candx, shard, up_in, down_in, sel, sel_t, stage, cols, target, terms, tin,
     up_out, up_sum, down_out, down_sum, fin, final_in, prebuf, topbuf, cbuf, cot,
     cand_s, cand_r, half_s, half_r, line_s, line_r, pull_s, pull_r, push_s, push_r,
@@ -145,8 +146,7 @@
     rows = 2 * stripe
     block = q_ref.shape[0]
     slots = teacher_ref.shape[1] // block
-    col = inp_ref.shape[1]
-    micro = inp_ref.shape[0]
+    micro, col = pre_ref.shape
     f32, bf16 = jnp.float32, jnp.bfloat16
 
     def remote(source, dest, send, recv, device):
@@ -166,6 +166,15 @@
             return carry
         lax.fori_loop(0, count, step, 0)
 
+    loads = [
+        pltpu.make_async_copy(source, dest, load_s.at[i])
+        for i, (source, dest) in enumerate(
+            ((q_hbm, q_ref), (teacher_hbm, teacher_ref), (w_hbm, w_ref))
+        )
+    ]
+    for load in loads:
+        load.start()
+
     barrier = pltpu.get_barrier_semaphore()
     everyone = 2 * dp_count
 
@@ -207,18 +216,20 @@
         line_copy(shard, down_in, 1, 0, -1).start()
 
     cand_copy.wait_recv()
-    pieces = []
-    for g in range(PLANE):
-        at = z * GROUP + (g // 4) * 2 + g % 2
-        mine = cand_ref[pl.ds(at, 1), :]
-        away = candx[pl.ds(at, 1), :]
-        row = jnp.where(section == (g // 2) % 2, mine, away)
-        pieces.append(jnp.broadcast_to(row.astype(f32), (slots * rows, row.shape[1])))
-    listed = jnp.concatenate(pieces, axis=0)
     total = PLANE * slots * rows
-    slot_of = (lax.broadcasted_iota(jnp.int32, listed.shape, 0) // rows) % slots
-    lane = lax.broadcasted_iota(jnp.int32, listed.shape, 1)
-    wanted = jnp.sum(jnp.where(lane == slot_of, listed, 0.0), axis=1, keepdims=True)
+    listed_shape = (total, dp_count)
+    at_row = lax.broadcasted_iota(jnp.int32, listed_shape, 0)
+    lane = lax.broadcasted_iota(jnp.int32, listed_shape, 1)
+    g_of = at_row // (slots * rows)
+    slot_of = (at_row // rows) % slots
+    here = (g_of // 2) % 2 == section
+    listed = jnp.zeros(listed_shape, f32)
+    for slot in range(slots):
+        mine = cand_ref[slot:slot + 1, :].astype(f32)
+        away = candx[slot:slot + 1, :].astype(f32)
+        listed = jnp.where(slot_of == slot, jnp.where(here, mine, away), listed)
+    picked_lane = lane == z * GROUP + (g_of // 4) * 2 + g_of % 2
+    wanted = jnp.sum(jnp.where(picked_lane, listed, 0.0), axis=1, keepdims=True)
     shape = (total, rows * block_total)
     row_of = lax.broadcasted_iota(jnp.int32, shape, 0) % rows
     place = lax.broadcasted_iota(jnp.int32, shape, 1)
@@ -252,7 +263,7 @@
 
     spread(shard, z)
 
-    prebuf[dp, :, :] = pre_ref[...]
+    prebuf[dp, :, :col] = pre_ref[...]
 
     def pre_copy(j):
         return remote(prebuf.at[dp], prebuf.at[dp], pre_s.at[j], pre_r.at[dp], (section, j))
@@ -265,12 +276,14 @@
         expons = jnp.where(valid, jnp.exp(masked - highest), 0.0)
         return expons / jnp.sum(expons, axis=-1, keepdims=True)
 
-    own_row = cand_ref[pl.ds(dp, 1), :].astype(f32)
+    own_row = count_ref[...].astype(f32)
     own_lane = lax.broadcasted_iota(jnp.int32, own_row.shape, 1)
-    how_many = jnp.sum(jnp.where(own_lane == slots, own_row, 0.0), axis=1, keepdims=True)
+    how_many = jnp.sum(jnp.where(own_lane == dp, own_row, 0.0), axis=1, keepdims=True)
     slot_lane = lax.broadcasted_iota(jnp.int32, teacher_ref.shape, 1) // block
     valid = slot_lane.astype(f32) < how_many
+    loads[1].wait()
     target[...] = soft(teacher_ref[...], valid)
+    loads[0].wait()
 
     for h in range(z_count - 1):
         @pl.when(z >= h + 1)
@@ -312,50 +325,50 @@
     weights = weights32.astype(bf16)
     weights_t = jnp.transpose(weights32).astype(bf16)
     for f in range(4):
+        sums = jnp.dot(
+            weights_t, q_ref[:, f * part:(f + 1) * part], preferred_element_type=f32
+        )
+        terms[f] = (sums * INVERSE_TEMP).astype(bf16).reshape(slots, block, part)
+
+    def push_copy(zt, g):
+        return remote(
+            terms.at[g % 4, :, own_rows(zt, g // 4), :], tin.at[zt, me],
+            push_s.at[zt, g], push_r.at[zt, me], member(g),
+        )
+
+    def push_wait(zt, g):
+        return remote(
+            terms.at[quarter, :, own_rows(zt, x), :], tin.at[zt, g],
+            push_s.at[zt, g], push_r.at[zt, g], member(g),
+        )
+
+    def push(zt):
+        others(PLANE, me, lambda g: push_copy(zt, g).start())
+        tin[zt, me] = terms[quarter, :, own_rows(zt, x), :]
+
+    bits = max(1, (z_count - 1).bit_length())
+    orders = [sorted(range(z_count), key=lambda t: (-abs(t - own), -t)) for own in range(z_count)]
+
+    def target_at(i):
+        code = sum(orders[own][i] << (bits * own) for own in range(z_count))
+        return lax.shift_right_logical(jnp.int32(code), (bits * z).astype(jnp.int32)) % (1 << bits)
+
+    push(target_at(0))
+    for f in range(4):
         sums = jnp.dot(weights, cols[f].reshape(slots * block, part), preferred_element_type=f32)
         sums = sums * INVERSE_TEMP
         qg_ref[:, f * part:(f + 1) * part] = sums.astype(bf16)
         topbuf[dp, :, f * part:(f + 1) * part] = sums[0:1]
 
+    qg_copy = pltpu.make_async_copy(qg_ref, qg_hbm, store_s.at[0])
+    qg_copy.start()
+
     def top_copy(j):
         return remote(topbuf.at[dp], topbuf.at[dp], top_s.at[j], top_r.at[dp], (section, j))
 
     @pl.when(section == 1)
     def _():
         others(dp_count, dp, lambda j: top_copy(j).start())
-
-    for f in range(4):
-        sums = jnp.dot(
-            weights_t, q_ref[:, f * part:(f + 1) * part], preferred_element_type=f32
-        )
-        terms[f] = (sums * INVERSE_TEMP).astype(bf16).reshape(slots, block, part)
-
-    def push_copy(zt, g):
-        return remote(
-            terms.at[g % 4, :, own_rows(zt, g // 4), :], tin.at[zt, me],
-            push_s.at[zt, g], push_r.at[zt, me], member(g),
-        )
-
-    def push_wait(zt, g):
-        return remote(
-            terms.at[quarter, :, own_rows(zt, x), :], tin.at[zt, g],
-            push_s.at[zt, g], push_r.at[zt, g], member(g),
-        )
-
-    def push(zt):
-        others(PLANE, me, lambda g: push_copy(zt, g).start())
-        tin[zt, me] = terms[quarter, :, own_rows(zt, x), :]
-
-    for h in range(z_count - 1, 0, -1):
-        @pl.when(z + h < z_count)
-        def _():
-            push(z + h)
-
-        @pl.when(z >= h)
-        def _():
-            push(z - h)
-
-    push(z)
 
     def cot_copy(j):
         return remote(cbuf.at[dp], cbuf.at[dp], cot_s.at[j], cot_r.at[dp], (1 - section, j))
@@ -367,21 +380,14 @@
         sigma = 1.0 / (1.0 + jnp.exp(-pre))
         slope = sigma * (1.0 + pre * (1.0 - sigma))
         inner = (cot[...] * slope).astype(bf16)
+        loads[2].wait()
         back = lax.dot_general(inner, w_ref[...], contract_last, preferred_element_type=f32)
         updated = own + back
         gi_ref[...] = updated
-        inner_parts = [(f, inner[:, f * part:(f + 1) * part]) for f in range(4)]
-
-        def outer():
-            for f, piece in inner_parts:
-                wg_ref[:, f * part:(f + 1) * part] = lax.dot_general(
-                    inp_ref[...], piece, contract_first, preferred_element_type=f32
-                ).astype(bf16)
-
-        return updated, outer
-
-    @pl.when(section == 1)
-    def _():
+        inner_ref[...] = inner
+        return updated
+
+    def last_section():
         others(dp_count, dp, lambda j: remote(
             topbuf.at[j], topbuf.at[j], top_s.at[j], top_r.at[j], (section, j)).wait_recv())
         own = jnp.zeros((micro, col), f32)
@@ -389,10 +395,9 @@
             cot[j:j + 1, :] = topbuf[j]
         for j in range(dp_count):
             own = jnp.where(dp == j, cot[:, j * col:(j + 1) * col], own)
-        updated, outer = layer(own)
+        updated = layer(own)
         cbuf[dp, :, :col] = updated
         others(dp_count, dp_count, lambda j: cot_copy(j).start())
-        outer()
 
     def summed(zt):
         others(PLANE, me, lambda g: push_wait(zt, g).wait_recv())
@@ -406,30 +411,36 @@
             (section, dp + step * GROUP),
         )
 
-    def line_sum(h, zt, step, sems, out, incoming, beyond):
-        value = summed(zt)
-        fin_shape = (rows, block_total, part)
-        out[h - 1] = value.astype(bf16).reshape(fin_shape)
-        if h < z_count - 1:
-            @pl.when(beyond)
-            def _():
-                sum_copy(out, incoming, sems, h, -step).wait_recv()
-                out[h - 1] = (value.reshape(fin_shape) + incoming[h].astype(f32)).astype(bf16)
+    def line_sum(value, h, step, sems, out, incoming, beyond):
+        out[h - 1] = value.astype(bf16)
+
+        @pl.when(beyond)
+        def _():
+            sum_copy(out, incoming, sems, h, -step).wait_recv()
+            out[h - 1] = (value + incoming[h].astype(f32)).astype(bf16)
+
         sum_copy(out, incoming, sems, h - 1, step).start()
 
-    for h in range(z_count - 1, 0, -1):
-        @pl.when(z + h < z_count)
-        def _():
-            line_sum(h, z + h, 1, 0, up_out, up_sum, z > 0)
-
-        @pl.when(z >= h)
-        def _():
-            line_sum(h, z - h, -1, 1, down_out, down_sum, z < z_count - 1)
+    for i in range(z_count - 1):
+        zt = target_at(i)
+        value = summed(zt).reshape(rows, block_total, part)
+        push(target_at(i + 1))
+
+        @pl.when(zt > z)
+        def _():
+            line_sum(value, zt - z, 1, 0, up_out, up_sum, z > 0)
+
+        @pl.when(zt < z)
+        def _():
+            line_sum(value, z - zt, -1, 1, down_out, down_sum, z < z_count - 1)
+
+        if i == 0:
+            pl.when(section == 1)(last_section)
 
     value = summed(z).reshape(rows, block_total, part)
 
     zero = jnp.zeros_like(value)
-    fin_acc = cot_like = None
+
     @pl.when(z > 0)
     def _():
         sum_copy(up_out, up_sum, 0, 0, -1).wait_recv()
@@ -464,13 +475,13 @@
             return carry
         lax.fori_loop(0, dp_count, wait, 0)
         cot[...] = jnp.concatenate([cbuf[j][:, :col] for j in range(dp_count)], axis=1)
-        updated, outer = layer(cbuf[dp][:, :col])
-        outer()
+        layer(cbuf[dp][:, :col])
 
     others(4, quarter, lambda i: fin_wait(i).wait_recv())
     for f in range(4):
         pg_ref[:, :, f * part:(f + 1) * part] = final_in[f]
 
+    qg_copy.wait()
     cand_copy.wait_send()
     half_copy.wait_send()
     for h in range(z_count - 1):
@@ -514,12 +525,15 @@
     micro, col = section_inputs.shape[1:]
     wide = -(-col // 128) * 128
     f32, bf16, i32 = jnp.float32, jnp.bfloat16, jnp.int32
-    table = jnp.concatenate([candidates, counts[:, None]], axis=1)
-    table = jnp.pad(table, ((0, 0), (0, 128 - slots - 1)))
-    pre = jnp.pad(pre_acts[0], ((0, 0), (0, wide - col)))
+    table = candidates.T
     vmem, dma = pltpu.VMEM, pltpu.SemaphoreType.DMA
     hop = z_count - 1
     scratch = [
+        vmem(queries.shape, bf16),
+        vmem(teacher.shape, f32),
+        vmem(section_weights.shape[1:], bf16),
+        vmem(queries.shape, bf16),
+        dma((3,)), dma((1,)),
         vmem(table.shape, i32),
         vmem((rows, block_total, part), bf16),
         vmem((hop, rows, block_total, part), bf16),
@@ -551,22 +565,25 @@
         dma((dp_count,)), dma((dp_count,)),
         dma((dp_count,)), dma((dp_count,)),
     ]
-    here = pl.BlockSpec(memory_space=vmem)
-    query_grads, passage_grads, grad_inputs, weight_grads = pl.pallas_call(
+    here, there = pl.BlockSpec(memory_space=vmem), pl.BlockSpec(memory_space=pl.ANY)
+    query_grads, passage_grads, grad_inputs, inner = pl.pallas_call(
         relay_kernel,
         out_shape=(
             jax.ShapeDtypeStruct(queries.shape, bf16),
             jax.ShapeDtypeStruct(passages.shape, bf16),
             jax.ShapeDtypeStruct((micro, col), f32),
-            jax.ShapeDtypeStruct(section_weights.shape[1:], bf16),
+            jax.ShapeDtypeStruct((micro, width), bf16),
         ),
-        in_specs=[here] * 7,
-        out_specs=(here,) * 4,
+        in_specs=[there, here, here, here, there, there, here],
+        out_specs=(there, here, here, here),
         scratch_shapes=scratch,
         compiler_params=pltpu.CompilerParams(
             collective_id=0, has_side_effects=True, vmem_limit_bytes=56 * 1024 * 1024
         ),
-    )(queries, passages, table, teacher, section_weights[0], section_inputs[0], pre)
+    )(queries, passages, table, counts[None], teacher, section_weights[0], pre_acts[0])
+    weight_grads = jnp.einsum(
+        "mi,mj->ij", section_inputs[0], inner, preferred_element_type=f32
+    ).astype(bf16)
     return query_grads, passage_grads, grad_inputs[None], weight_grads[None]
 
 

time: 130 us -> 126 us (0.969)
  local copies, waits for them, and re-layouts: 7 us -> 2.47 us
  matrix products: 0 us -> 2.8 us
    dot_general x0 -> x1, matrix products: none -> 2.8 us  [plane_body(): jnp.einsum('mi,mj->ij', section_inputs[0], inner, preferred_element_type=...]
    unnamed x10 -> x11, local copies, waits for them, and re-layouts: 5 us -> 2.47 us
    pad x2 -> x0, local copies, waits for them, and re-layouts: 1.91 us -> none  [the longest x1 1.3 us: plane_body(): pre = jnp.pad(pre_acts[0], ((0, 0), (0, wide - col)))]
where the time goes in v2:
time: 126 us
  Pallas kernels  120 us (95%)
  matrix products  2.8 us (2%)
  local copies, waits for them, and re-layouts  2.47 us (2%)
    pallas_call x1, Pallas kernels, plane_body(): pl.pallas_call(relay_kernel, out_shape=(jax.ShapeDtypeStruct(queries.shap...  120 us
    dot_general x1, matrix products, plane_body(): jnp.einsum('mi,mj->ij', section_inputs[0], inner, preferred_element_type=...  2.8 us

profile of v2, /device:TPU:1, one launch (start us, length us, event | category | flops | bytes accessed | tf_op | source)
XLA Modules:
  0.0 126.2 jit_solution(8162016015994901688)
XLA Ops:
  0.6 0.0 copy-start
  0.6 120.2 %shard_map.111 = (bf16[128,3584]{1,0:T(8,128)(2,1)}, bf16[8,16,3584]{2,1,0:T(8,128)(2,1)}, f32[16,224]{1,0:T(8,128)}, bf16[16,3584]{1,0:T(8,128)(2,1)}) custom-call(bf16[128,3584]{1,0:T(8,128)(2,1)} %q_hbm.1, bf16[8,16,3584]{2,1,0:T(8,128)(2,1)} %p_ref.1, s32[3,16]{1,0:T(4,128)} %bitcast.16, s32[1,16]{1,0:T(1,128)} %bitcast.17, f32[128,384]{1,0:T(8,128)} %teacher_hbm.1, ...), custom_call_target="tpu_custom_call" | custom-call | tf_op jit(solution)/shard_map/pallas_call | solution.py:569
  120.9 0.0 copy-start.2
  120.9 0.0 copy-done
  120.9 0.0 copy-start.1
  120.9 2.8 %fusion = bf16[1,224,3584]{2,1,0:T(8,128)(2,1)} fusion(bf16[16,3584]{1,0:T(8,128)(2,1)} %get-tuple-element.11, bf16[1,16,224]{2,1,0:T(8,128)(2,1)S(1)} %copy-done), kind=kOutput, calls=%fused_computation.1 | convolution fusion | flops 26492928 | bytes 1727488 | tf_op jit(solution)/shard_map/mi,mj->ij/dot_general | solution.py:584
  123.7 0.0 copy-done.2
  123.7 0.0 copy-start.3
  123.7 0.9 copy.15
  124.6 0.0 copy-done.1
  124.6 0.9 copy.16
  125.6 0.0 copy-done.3
  125.6 0.6 copy.17
Async XLA Ops:
  0.6 120.3 %copy-start = (bf16[1,16,224]{2,1,0:T(8,128)(2,1)S(1)}, bf16[1,16,224]{2,1,0:T(8,128)(2,1)}, u32[]{:S(2)}) copy-start(bf16[1,16,224]{2,1,0:T(8,128)(2,1)} %param.14) | copy-start | bytes 21508
  120.9 2.8 %copy-start.2 = (bf16[128,3584]{1,0:T(8,128)(2,1)S(1)}, bf16[128,3584]{1,0:T(8,128)(2,1)}, u32[]{:S(2)}) copy-start(bf16[128,3584]{1,0:T(8,128)(2,1)} %get-tuple-element.16) | copy-start | bytes 2752516
  120.9 3.7 %copy-start.1 = (bf16[8,16,3584]{2,1,0:T(8,128)(2,1)S(1)}, bf16[8,16,3584]{2,1,0:T(8,128)(2,1)}, u32[]{:S(2)}) copy-start(bf16[8,16,3584]{2,1,0:T(8,128)(2,1)} %get-tuple-element.17) | copy-start | bytes 2752516
  123.7 1.9 %copy-start.3 = (f32[16,224]{1,0:T(8,128)S(1)}, f32[16,224]{1,0:T(8,128)}, u32[]{:S(2)}) copy-start(f32[16,224]{1,0:T(8,128)} %get-tuple-element.10) | copy-start | bytes 43012

commit v3 on v2

--- a/solution.py
+++ b/solution.py
@@ -119,6 +119,17 @@
 GROUP = 4
 
 
+def chunks_of(width, count):
+    lanes, edges = width // 128, [0]
+    for i in range(count):
+        edges.append(edges[-1] + -(-(lanes - edges[-1]) // (count - i)))
+    return [(128 * a, 128 * (b - a)) for a, b in zip(edges, edges[1:])]
+
+
+CHUNKS = 2
+AHEAD = 2
+
+
 def cells(width, ref, index):
     return ref.at[:, :, pl.ds(pl.multiple_of(index * width, width), width)]
 
@@ -126,7 +137,7 @@
 def relay_kernel(
     q_hbm, p_ref, cand_ref, count_ref, teacher_hbm, w_hbm, pre_ref,
     qg_hbm, pg_ref, gi_ref, inner_ref,
-    q_ref, teacher_ref, w_ref, qg_ref, load_s, store_s,
+    q_ref, teacher_ref, w_ref, qg_ref, slope_ref, load_s, store_s,
     candx, shard, up_in, down_in, sel, sel_t, stage, cols, target, terms, tin,
     up_out, up_sum, down_out, down_sum, fin, final_in, prebuf, topbuf, cbuf, cot,
     cand_s, cand_r, half_s, half_r, line_s, line_r, pull_s, pull_r, push_s, push_r,
@@ -148,6 +159,10 @@
     slots = teacher_ref.shape[1] // block
     micro, col = pre_ref.shape
     f32, bf16 = jnp.float32, jnp.bfloat16
+    chunks = chunks_of(part, CHUNKS)
+
+    def lanes(c):
+        return pl.ds(*chunks[c])
 
     def remote(source, dest, send, recv, device):
         return pltpu.make_async_remote_copy(
@@ -204,16 +219,21 @@
     )
     half_wait.wait_recv()
 
-    def line_copy(source, ref, sems, h, step):
-        return remote(source, ref.at[h], line_s.at[sems, h], line_r.at[sems, h], (section, dp + step * GROUP))
+    def line_copy(source, ref, sems, h, c, step):
+        return remote(
+            source.at[:, :, lanes(c)], ref.at[h, :, :, lanes(c)],
+            line_s.at[sems, h, c], line_r.at[sems, h, c], (section, dp + step * GROUP),
+        )
 
     @pl.when(z < z_count - 1)
     def _():
-        line_copy(shard, up_in, 0, 0, 1).start()
+        for c in range(CHUNKS):
+            line_copy(shard, up_in, 0, 0, c, 1).start()
 
     @pl.when(z > 0)
     def _():
-        line_copy(shard, down_in, 1, 0, -1).start()
+        for c in range(CHUNKS):
+            line_copy(shard, down_in, 1, 0, c, -1).start()
 
     cand_copy.wait_recv()
     total = PLANE * slots * rows
@@ -241,27 +261,30 @@
     def own_rows(zs, at_x):
         return pl.ds(pl.multiple_of(zs * GROUP * stripe + at_x * rows, rows), rows)
 
-    def pull_copy(zs, g):
+    def pull_copy(zs, g, c):
         return remote(
-            stage.at[zs, g], cols.at[quarter, :, own_rows(zs, x), :],
-            pull_s.at[zs, g], pull_r.at[zs, me], member(g),
-        )
-
-    def pull_wait(zs, g):
+            stage.at[zs, g, :, :, lanes(c)], cols.at[quarter, :, own_rows(zs, x), lanes(c)],
+            pull_s.at[zs, g, c], pull_r.at[zs, me, c], member(g),
+        )
+
+    def pull_wait(zs, g, c):
         return remote(
-            stage.at[zs, g], cols.at[g % 4, :, own_rows(zs, g // 4), :],
-            pull_s.at[zs, g], pull_r.at[zs, g], member(g),
-        )
-
-    def spread(ref, zs):
+            stage.at[zs, g, :, :, lanes(c)], cols.at[g % 4, :, own_rows(zs, g // 4), lanes(c)],
+            pull_s.at[zs, g, c], pull_r.at[zs, g, c], member(g),
+        )
+
+    def spread(ref, zs, c):
+        size = chunks[c][1]
         picked = jnp.dot(
-            sel[...], ref[...].reshape(rows * block_total, part), preferred_element_type=f32
-        )
-        stage[zs] = picked.astype(bf16).reshape(PLANE, slots, rows, part)
-        others(PLANE, me, lambda g: pull_copy(zs, g).start())
-        cols[quarter, :, own_rows(zs, x), :] = stage[zs, me]
-
-    spread(shard, z)
+            sel[...], ref[:, :, lanes(c)].reshape(rows * block_total, size),
+            preferred_element_type=f32,
+        )
+        stage[zs, :, :, :, lanes(c)] = picked.astype(bf16).reshape(PLANE, slots, rows, size)
+        others(PLANE, me, lambda g: pull_copy(zs, g, c).start())
+        cols[quarter, :, own_rows(zs, x), lanes(c)] = stage[zs, me, :, :, lanes(c)]
+
+    for c in range(CHUNKS):
+        spread(shard, z, c)
 
     prebuf[dp, :, :col] = pre_ref[...]
 
@@ -285,75 +308,93 @@
     target[...] = soft(teacher_ref[...], valid)
     loads[0].wait()
 
-    for h in range(z_count - 1):
+    def slopes():
+        others(dp_count, dp, lambda j: remote(
+            prebuf.at[j], prebuf.at[j], pre_s.at[j], pre_r.at[j], (section, j)).wait_recv())
+        pre = jnp.concatenate([prebuf[j].astype(f32)[:, :col] for j in range(dp_count)], axis=1)
+        sigma = 1.0 / (1.0 + jnp.exp(-pre))
+        slope_ref[...] = sigma * (1.0 + pre * (1.0 - sigma))
+
+    def hop(h, c):
         @pl.when(z >= h + 1)
         def _():
-            line_copy(shard, up_in, 0, h, -1).wait_recv()
+            line_copy(shard, up_in, 0, h, c, -1).wait_recv()
             if h + 1 < z_count - 1:
                 @pl.when(z < z_count - 1)
                 def _():
-                    line_copy(up_in.at[h], up_in, 0, h + 1, 1).start()
+                    line_copy(up_in.at[h], up_in, 0, h + 1, c, 1).start()
 
         @pl.when(z + h + 1 < z_count)
         def _():
-            line_copy(shard, down_in, 1, h, 1).wait_recv()
+            line_copy(shard, down_in, 1, h, c, 1).wait_recv()
             if h + 1 < z_count - 1:
                 @pl.when(z > 0)
                 def _():
-                    line_copy(down_in.at[h], down_in, 1, h + 1, -1).start()
+                    line_copy(down_in.at[h], down_in, 1, h + 1, c, -1).start()
 
         @pl.when(z >= h + 1)
         def _():
-            spread(up_in.at[h], z - h - 1)
+            spread(up_in.at[h], z - h - 1, c)
 
         @pl.when(z + h + 1 < z_count)
         def _():
-            spread(down_in.at[h], z + h + 1)
-
-    for zs in range(z_count):
-        others(PLANE, me, lambda g: pull_wait(zs, g).wait_recv())
+            spread(down_in.at[h], z + h + 1, c)
+
+    for h in range(z_count - 1):
+        if h == z_count - 2:
+            slopes()
+        for c in range(CHUNKS):
+            hop(h, c)
 
     contract_last = (((1,), (1,)), ((), ()))
-    contract_first = (((0,), (0,)), ((), ()))
     logits = jnp.zeros((block, slots * block), f32)
-    for f in range(4):
-        logits += lax.dot_general(
-            q_ref[:, f * part:(f + 1) * part], cols[f].reshape(slots * block, part),
-            contract_last, preferred_element_type=f32,
-        )
+    for c, (offset, size) in enumerate(chunks):
+        for zs in range(z_count):
+            others(PLANE, me, lambda g: pull_wait(zs, g, c).wait_recv())
+        for f in range(4):
+            logits += lax.dot_general(
+                q_ref[:, f * part + offset:f * part + offset + size],
+                cols[f, :, :, lanes(c)].reshape(slots * block, size),
+                contract_last, preferred_element_type=f32,
+            )
     weights32 = soft(logits * INVERSE_TEMP, valid) - target[...]
     weights = weights32.astype(bf16)
     weights_t = jnp.transpose(weights32).astype(bf16)
-    for f in range(4):
-        sums = jnp.dot(
-            weights_t, q_ref[:, f * part:(f + 1) * part], preferred_element_type=f32
-        )
-        terms[f] = (sums * INVERSE_TEMP).astype(bf16).reshape(slots, block, part)
-
-    def push_copy(zt, g):
+    def push_copy(zt, g, c):
         return remote(
-            terms.at[g % 4, :, own_rows(zt, g // 4), :], tin.at[zt, me],
-            push_s.at[zt, g], push_r.at[zt, me], member(g),
-        )
-
-    def push_wait(zt, g):
+            terms.at[g % 4, :, own_rows(zt, g // 4), lanes(c)], tin.at[zt, me, :, :, lanes(c)],
+            push_s.at[zt, g, c], push_r.at[zt, me, c], member(g),
+        )
+
+    def push_wait(zt, g, c):
         return remote(
-            terms.at[quarter, :, own_rows(zt, x), :], tin.at[zt, g],
-            push_s.at[zt, g], push_r.at[zt, g], member(g),
-        )
-
-    def push(zt):
-        others(PLANE, me, lambda g: push_copy(zt, g).start())
-        tin[zt, me] = terms[quarter, :, own_rows(zt, x), :]
+            terms.at[quarter, :, own_rows(zt, x), lanes(c)], tin.at[zt, g, :, :, lanes(c)],
+            push_s.at[zt, g, c], push_r.at[zt, g, c], member(g),
+        )
+
+    def push(zt, c):
+        others(PLANE, me, lambda g: push_copy(zt, g, c).start())
+        tin[zt, me, :, :, lanes(c)] = terms[quarter, :, own_rows(zt, x), lanes(c)]
 
     bits = max(1, (z_count - 1).bit_length())
-    orders = [sorted(range(z_count), key=lambda t: (-abs(t - own), -t)) for own in range(z_count)]
+    orders = [sorted(range(z_count), key=lambda t: (-abs(t - own), -abs(2 * t - z_count + 1))) for own in range(z_count)]
 
     def target_at(i):
         code = sum(orders[own][i] << (bits * own) for own in range(z_count))
         return lax.shift_right_logical(jnp.int32(code), (bits * z).astype(jnp.int32)) % (1 << bits)
 
-    push(target_at(0))
+    turns = [(i, c) for i in range(z_count) for c in range(CHUNKS)]
+    for c, (offset, size) in enumerate(chunks):
+        for f in range(4):
+            sums = jnp.dot(
+                weights_t, q_ref[:, f * part + offset:f * part + offset + size],
+                preferred_element_type=f32,
+            )
+            terms[f, :, :, lanes(c)] = (
+                (sums * INVERSE_TEMP).astype(bf16).reshape(slots, block, size)
+            )
+        if c < AHEAD:
+            push(target_at(0), c)
     for f in range(4):
         sums = jnp.dot(weights, cols[f].reshape(slots * block, part), preferred_element_type=f32)
         sums = sums * INVERSE_TEMP
@@ -374,12 +415,7 @@
         return remote(cbuf.at[dp], cbuf.at[dp], cot_s.at[j], cot_r.at[dp], (1 - section, j))
 
     def layer(own):
-        others(dp_count, dp, lambda j: remote(
-            prebuf.at[j], prebuf.at[j], pre_s.at[j], pre_r.at[j], (section, j)).wait_recv())
-        pre = jnp.concatenate([prebuf[j].astype(f32)[:, :col] for j in range(dp_count)], axis=1)
-        sigma = 1.0 / (1.0 + jnp.exp(-pre))
-        slope = sigma * (1.0 + pre * (1.0 - sigma))
-        inner = (cot[...] * slope).astype(bf16)
+        inner = (cot[...] * slope_ref[...]).astype(bf16)
         loads[2].wait()
         back = lax.dot_general(inner, w_ref[...], contract_last, preferred_element_type=f32)
         updated = own + back
@@ -399,74 +435,80 @@
         cbuf[dp, :, :col] = updated
         others(dp_count, dp_count, lambda j: cot_copy(j).start())
 
-    def summed(zt):
-        others(PLANE, me, lambda g: push_wait(zt, g).wait_recv())
+    def summed(zt, c):
+        others(PLANE, me, lambda g: push_wait(zt, g, c).wait_recv())
+        size = chunks[c][1]
         return jnp.dot(
-            sel_t[...], tin[zt].reshape(total, part), preferred_element_type=f32
-        )
-
-    def sum_copy(source, dest, sems, h, step):
+            sel_t[...], tin[zt, :, :, :, lanes(c)].reshape(total, size),
+            preferred_element_type=f32,
+        ).reshape(rows, block_total, size)
+
+    def sum_copy(source, dest, sems, h, c, step):
         return remote(
-            source.at[h], dest.at[h], sum_s.at[sems, h], sum_r.at[sems, h],
-            (section, dp + step * GROUP),
-        )
-
-    def line_sum(value, h, step, sems, out, incoming, beyond):
-        out[h - 1] = value.astype(bf16)
+            source.at[h, :, :, lanes(c)], dest.at[h, :, :, lanes(c)],
+            sum_s.at[sems, h, c], sum_r.at[sems, h, c], (section, dp + step * GROUP),
+        )
+
+    def line_sum(value, h, c, step, sems, out, incoming, beyond):
+        out[h - 1, :, :, lanes(c)] = value.astype(bf16)
 
         @pl.when(beyond)
         def _():
-            sum_copy(out, incoming, sems, h, -step).wait_recv()
-            out[h - 1] = (value + incoming[h].astype(f32)).astype(bf16)
-
-        sum_copy(out, incoming, sems, h - 1, step).start()
-
-    for i in range(z_count - 1):
+            sum_copy(out, incoming, sems, h, c, -step).wait_recv()
+            both = value + incoming[h, :, :, lanes(c)].astype(f32)
+            out[h - 1, :, :, lanes(c)] = both.astype(bf16)
+
+        sum_copy(out, incoming, sems, h - 1, c, step).start()
+
+    def fin_copy(i, c):
+        return remote(
+            fin.at[pl.ds((i % 2) * stripe, stripe), :, lanes(c)],
+            final_in.at[quarter, :, :, lanes(c)],
+            fin_s.at[i, c], fin_r.at[quarter, c], (i // 2, z * GROUP + x * 2 + i % 2),
+        )
+
+    def fin_wait(i, c):
+        return remote(
+            fin.at[pl.ds(core * stripe, stripe), :, lanes(c)], final_in.at[i, :, :, lanes(c)],
+            fin_s.at[i, c], fin_r.at[i, c], (i // 2, z * GROUP + x * 2 + i % 2),
+        )
+
+    def own_sum(value, c):
+        zero = jnp.zeros_like(value)
+
+        @pl.when(z > 0)
+        def _():
+            sum_copy(up_out, up_sum, 0, 0, c, -1).wait_recv()
+
+        @pl.when(z < z_count - 1)
+        def _():
+            sum_copy(down_out, down_sum, 1, 0, c, 1).wait_recv()
+
+        below = jnp.where(z > 0, up_sum[0, :, :, lanes(c)].astype(f32), zero)
+        above = jnp.where(z < z_count - 1, down_sum[0, :, :, lanes(c)].astype(f32), zero)
+        fin[:, :, lanes(c)] = (value + below + above).astype(bf16)
+        others(4, quarter, lambda i: fin_copy(i, c).start())
+        final_in[quarter, :, :, lanes(c)] = fin[pl.ds(core * stripe, stripe), :, lanes(c)]
+
+    for turn, (i, c) in enumerate(turns):
         zt = target_at(i)
-        value = summed(zt).reshape(rows, block_total, part)
-        push(target_at(i + 1))
+        value = summed(zt, c)
+        if turn + AHEAD < len(turns):
+            push(target_at(turns[turn + AHEAD][0]), turns[turn + AHEAD][1])
+        if i == z_count - 1:
+            own_sum(value, c)
+            continue
 
         @pl.when(zt > z)
         def _():
-            line_sum(value, zt - z, 1, 0, up_out, up_sum, z > 0)
+            line_sum(value, zt - z, c, 1, 0, up_out, up_sum, z > 0)
 
         @pl.when(zt < z)
         def _():
-            line_sum(value, z - zt, -1, 1, down_out, down_sum, z < z_count - 1)
-
-        if i == 0:
+            line_sum(value, z - zt, c, -1, 1, down_out, down_sum, z < z_count - 1)
+
+        if turn == CHUNKS:
             pl.when(section == 1)(last_section)
-
-    value = summed(z).reshape(rows, block_total, part)
-
-    zero = jnp.zeros_like(value)
-
-    @pl.when(z > 0)
-    def _():
-        sum_copy(up_out, up_sum, 0, 0, -1).wait_recv()
-
-    @pl.when(z < z_count - 1)
-    def _():
-        sum_copy(down_out, down_sum, 1, 0, 1).wait_recv()
-
-    below = jnp.where(z > 0, up_sum[0].astype(f32), zero)
-    above = jnp.where(z < z_count - 1, down_sum[0].astype(f32), zero)
-    fin[...] = (value + below + above).astype(bf16)
-
-    def fin_copy(i):
-        return remote(
-            fin.at[pl.ds((i % 2) * stripe, stripe)], final_in.at[quarter],
-            fin_s.at[i], fin_r.at[quarter], (i // 2, z * GROUP + x * 2 + i % 2),
-        )
-
-    def fin_wait(i):
-        return remote(
-            fin.at[pl.ds(core * stripe, stripe)], final_in.at[i],
-            fin_s.at[i], fin_r.at[i], (i // 2, z * GROUP + x * 2 + i % 2),
-        )
-
-    others(4, quarter, lambda i: fin_copy(i).start())
-    final_in[quarter] = fin[pl.ds(core * stripe, stripe)]
 
     @pl.when(section == 0)
     def _():
@@ -477,7 +519,8 @@
         cot[...] = jnp.concatenate([cbuf[j][:, :col] for j in range(dp_count)], axis=1)
         layer(cbuf[dp][:, :col])
 
-    others(4, quarter, lambda i: fin_wait(i).wait_recv())
+    for c in range(CHUNKS):
+        others(4, quarter, lambda i: fin_wait(i, c).wait_recv())
     for f in range(4):
         pg_ref[:, :, f * part:(f + 1) * part] = final_in[f]
 
@@ -485,25 +528,30 @@
     cand_copy.wait_send()
     half_copy.wait_send()
     for h in range(z_count - 1):
-        @pl.when((z >= h) & (z < z_count - 1))
-        def _():
-            line_copy(up_in.at[h], up_in, 0, h, 1).wait_send()
-
-        @pl.when((z + h < z_count) & (z > 0))
-        def _():
-            line_copy(down_in.at[h], down_in, 1, h, -1).wait_send()
-
-        @pl.when(z + h + 1 < z_count)
-        def _():
-            sum_copy(up_out, up_sum, 0, h, 1).wait_send()
-
-        @pl.when(z >= h + 1)
-        def _():
-            sum_copy(down_out, down_sum, 1, h, -1).wait_send()
-
-    for zs in range(z_count):
-        others(PLANE, me, lambda g: pull_copy(zs, g).wait_send())
-        others(PLANE, me, lambda g: push_copy(zs, g).wait_send())
+        for c in range(CHUNKS):
+            @pl.when((z >= h) & (z < z_count - 1))
+            def _():
+                line_copy(up_in.at[h], up_in, 0, h, c, 1).wait_send()
+
+            @pl.when((z + h < z_count) & (z > 0))
+            def _():
+                line_copy(down_in.at[h], down_in, 1, h, c, -1).wait_send()
+
+            @pl.when(z + h + 1 < z_count)
+            def _():
+                sum_copy(up_out, up_sum, 0, h, c, 1).wait_send()
+
+            @pl.when(z >= h + 1)
+            def _():
+                sum_copy(down_out, down_sum, 1, h, c, -1).wait_send()
+
+    def sent(zs, carry):
+        for c in range(CHUNKS):
+            others(PLANE, me, lambda g: pull_copy(zs, g, c).wait_send())
+            others(PLANE, me, lambda g: push_copy(zs, g, c).wait_send())
+        return carry
+
+    lax.fori_loop(0, z_count, sent, 0)
     others(dp_count, dp, lambda j: pre_copy(j).wait_send())
 
     @pl.when(section == 1)
@@ -511,7 +559,26 @@
         others(dp_count, dp, lambda j: top_copy(j).wait_send())
         others(dp_count, dp_count, lambda j: cot_copy(j).wait_send())
 
-    others(4, quarter, lambda i: fin_copy(i).wait_send())
+    for c in range(CHUNKS):
+        others(4, quarter, lambda i: fin_copy(i, c).wait_send())
+
+
+def finish_kernel(qg_in, pg_in, gi_in, inner_ref, inp_ref, qg_ref, pg_ref, gi_ref, wg_ref, sems):
+    copies = [
+        pltpu.make_async_copy(qg_in, qg_ref, sems.at[0]),
+        pltpu.make_async_copy(pg_in, pg_ref, sems.at[1]),
+    ]
+    for copy in copies:
+        copy.start()
+    gi_ref[...] = gi_in[...]
+    part = inner_ref.shape[1] // 4
+    for f in range(4):
+        wg_ref[:, f * part:(f + 1) * part] = lax.dot_general(
+            inp_ref[...], inner_ref[:, f * part:(f + 1) * part],
+            (((0,), (0,)), ((), ())), preferred_element_type=jnp.float32,
+        ).astype(wg_ref.dtype)
+    for copy in copies:
+        copy.wait()
 
 
 def plane_body(queries, passages, candidates, counts, teacher, section_weights, section_inputs, pre_acts):
@@ -533,6 +600,7 @@
         vmem(teacher.shape, f32),
         vmem(section_weights.shape[1:], bf16),
         vmem(queries.shape, bf16),
+        vmem((micro, width), f32),
         dma((3,)), dma((1,)),
         vmem(table.shape, i32),
         vmem((rows, block_total, part), bf16),
@@ -556,11 +624,11 @@
         vmem((dp_count, micro, wide), f32),
         vmem((micro, width), f32),
         dma((1,)), dma((1,)), dma((1,)), dma((1,)),
-        dma((2, hop)), dma((2, hop)),
-        dma((z_count, PLANE)), dma((z_count, PLANE)),
-        dma((z_count, PLANE)), dma((z_count, PLANE)),
-        dma((2, hop)), dma((2, hop)),
-        dma((4,)), dma((4,)),
+        dma((2, hop, CHUNKS)), dma((2, hop, CHUNKS)),
+        dma((z_count, PLANE, CHUNKS)), dma((z_count, PLANE, CHUNKS)),
+        dma((z_count, PLANE, CHUNKS)), dma((z_count, PLANE, CHUNKS)),
+        dma((2, hop, CHUNKS)), dma((2, hop, CHUNKS)),
+        dma((4, CHUNKS)), dma((4, CHUNKS)),
         dma((dp_count,)), dma((dp_count,)),
         dma((dp_count,)), dma((dp_count,)),
         dma((dp_count,)), dma((dp_count,)),
@@ -581,9 +649,19 @@
             collective_id=0, has_side_effects=True, vmem_limit_bytes=56 * 1024 * 1024
         ),
     )(queries, passages, table, counts[None], teacher, section_weights[0], pre_acts[0])
-    weight_grads = jnp.einsum(
-        "mi,mj->ij", section_inputs[0], inner, preferred_element_type=f32
-    ).astype(bf16)
+    query_grads, passage_grads, grad_inputs, weight_grads = pl.pallas_call(
+        finish_kernel,
+        out_shape=(
+            jax.ShapeDtypeStruct(queries.shape, bf16),
+            jax.ShapeDtypeStruct(passages.shape, bf16),
+            jax.ShapeDtypeStruct((micro, col), f32),
+            jax.ShapeDtypeStruct(section_weights.shape[1:], bf16),
+        ),
+        in_specs=[there, there, here, here, here],
+        out_specs=(there, there, here, here),
+        scratch_shapes=[dma((2,))],
+        compiler_params=pltpu.CompilerParams(vmem_limit_bytes=60 * 1024 * 1024),
+    )(query_grads, passage_grads, grad_inputs, inner, section_inputs[0])
     return query_grads, passage_grads, grad_inputs[None], weight_grads[None]
 
 

time: 126 us -> 166 us (1.32)
  the two profiles are of different devices: /device:TPU:1 before, /device:TPU:13 now
where the time goes in v3:
time: 166 us
  Pallas kernels  165 us (99%)
    pallas_call x1, Pallas kernels, plane_body(): pl.pallas_call(relay_kernel, out_shape=(jax.ShapeDtypeStruct(queries.shap...  106 us
    pallas_call x1, Pallas kernels, plane_body(): pl.pallas_call(finish_kernel, out_shape=(jax.ShapeDtypeStruct(queries.sha...  58.8 us

profile of v3, /device:TPU:13, one launch (start us, length us, event | category | flops | bytes accessed | tf_op | source)
XLA Modules:
  0.0 165.9 jit_solution(3994706994368525244)
XLA Ops:
  0.6 106.5 %shard_map.111 = (bf16[128,3584]{1,0:T(8,128)(2,1)}, bf16[8,16,3584]{2,1,0:T(8,128)(2,1)}, f32[16,224]{1,0:T(8,128)}, bf16[16,3584]{1,0:T(8,128)(2,1)}) custom-call(bf16[128,3584]{1,0:T(8,128)(2,1)} %q_hbm.1, bf16[8,16,3584]{2,1,0:T(8,128)(2,1)} %p_ref.1, s32[3,16]{1,0:T(4,128)} %bitcast.10, s32[1,16]{1,0:T(1,128)} %bitcast.11, f32[128,384]{1,0:T(8,128)} %teacher_hbm.1, ...), custom_call_target="tpu_custom_call" | custom-call | tf_op jit(solution)/shard_map/pallas_call | solution.py:637
  107.1 58.8 %shard_map.112 = (bf16[128,3584]{1,0:T(8,128)(2,1)}, bf16[8,16,3584]{2,1,0:T(8,128)(2,1)}, f32[16,224]{1,0:T(8,128)}, bf16[224,3584]{1,0:T(8,128)(2,1)}) custom-call(bf16[128,3584]{1,0:T(8,128)(2,1)} %get-tuple-element.12.qg_in, bf16[8,16,3584]{2,1,0:T(8,128)(2,1)} %get-tuple-element.13.pg_in, f32[16,224]{1,0:T(8,128)} %get-tuple-element.14.gi_in, ...), custom_call_target="tpu_custom_call" | custom-call | tf_op jit(solution)/shard_map/pallas_call | solution.py:652

commit v4 on v3

--- a/solution.py
+++ b/solution.py
@@ -126,8 +126,8 @@
     return [(128 * a, 128 * (b - a)) for a, b in zip(edges, edges[1:])]
 
 
-CHUNKS = 2
-AHEAD = 2
+CHUNKS = 3
+AHEAD = 3
 
 
 def cells(width, ref, index):
@@ -175,9 +175,24 @@
 
     def others(count, own, act):
         def step(i, carry):
-            @pl.when(i != own)
-            def _():
-                act(i)
+            act((own + i) % count)
+            return carry
+        lax.fori_loop(1, count, step, 0)
+
+    def peers(act):
+        def step(j, carry):
+            i = (j * 5) % PLANE
+            act(
+                (x + i // 4) % 2 * 4
+                + (section + (i // 2) % 2) % 2 * 2
+                + (core + i % 2) % 2
+            )
+            return carry
+        lax.fori_loop(1, PLANE, step, 0)
+
+    def each(count, act):
+        def step(i, carry):
+            act(i)
             return carry
         lax.fori_loop(0, count, step, 0)
 
@@ -280,7 +295,7 @@
             preferred_element_type=f32,
         )
         stage[zs, :, :, :, lanes(c)] = picked.astype(bf16).reshape(PLANE, slots, rows, size)
-        others(PLANE, me, lambda g: pull_copy(zs, g, c).start())
+        peers(lambda g: pull_copy(zs, g, c).start())
         cols[quarter, :, own_rows(zs, x), lanes(c)] = stage[zs, me, :, :, lanes(c)]
 
     for c in range(CHUNKS):
@@ -350,7 +365,7 @@
     logits = jnp.zeros((block, slots * block), f32)
     for c, (offset, size) in enumerate(chunks):
         for zs in range(z_count):
-            others(PLANE, me, lambda g: pull_wait(zs, g, c).wait_recv())
+            peers(lambda g: pull_wait(zs, g, c).wait_recv())
         for f in range(4):
             logits += lax.dot_general(
                 q_ref[:, f * part + offset:f * part + offset + size],
@@ -373,7 +388,7 @@
         )
 
     def push(zt, c):
-        others(PLANE, me, lambda g: push_copy(zt, g, c).start())
+        peers(lambda g: push_copy(zt, g, c).start())
         tin[zt, me, :, :, lanes(c)] = terms[quarter, :, own_rows(zt, x), lanes(c)]
 
     bits = max(1, (z_count - 1).bit_length())
@@ -433,10 +448,10 @@
             own = jnp.where(dp == j, cot[:, j * col:(j + 1) * col], own)
         updated = layer(own)
         cbuf[dp, :, :col] = updated
-        others(dp_count, dp_count, lambda j: cot_copy(j).start())
+        each(dp_count, lambda j: cot_copy(j).start())
 
     def summed(zt, c):
-        others(PLANE, me, lambda g: push_wait(zt, g, c).wait_recv())
+        peers(lambda g: push_wait(zt, g, c).wait_recv())
         size = chunks[c][1]
         return jnp.dot(
             sel_t[...], tin[zt, :, :, :, lanes(c)].reshape(total, size),
@@ -547,8 +562,8 @@
 
     def sent(zs, carry):
         for c in range(CHUNKS):
-            others(PLANE, me, lambda g: pull_copy(zs, g, c).wait_send())
-            others(PLANE, me, lambda g: push_copy(zs, g, c).wait_send())
+            peers(lambda g: pull_copy(zs, g, c).wait_send())
+            peers(lambda g: push_copy(zs, g, c).wait_send())
         return carry
 
     lax.fori_loop(0, z_count, sent, 0)
@@ -557,28 +572,42 @@
     @pl.when(section == 1)
     def _():
         others(dp_count, dp, lambda j: top_copy(j).wait_send())
-        others(dp_count, dp_count, lambda j: cot_copy(j).wait_send())
+        each(dp_count, lambda j: cot_copy(j).wait_send())
 
     for c in range(CHUNKS):
         others(4, quarter, lambda i: fin_copy(i, c).wait_send())
 
 
-def finish_kernel(qg_in, pg_in, gi_in, inner_ref, inp_ref, qg_ref, pg_ref, gi_ref, wg_ref, sems):
-    copies = [
-        pltpu.make_async_copy(qg_in, qg_ref, sems.at[0]),
-        pltpu.make_async_copy(pg_in, pg_ref, sems.at[1]),
+def finish_kernel(
+    qg_in, pg_in, gi_in, inner_ref, inp_ref, qg_out, pg_out, gi_ref, wg_out,
+    qg, pg, wg, in_s, out_s,
+):
+    held = (qg, pg)
+    takes = [
+        pltpu.make_async_copy(source, ref, in_s.at[i])
+        for i, (source, ref) in enumerate(zip((qg_in, pg_in), held))
     ]
-    for copy in copies:
-        copy.start()
+    gives = [
+        pltpu.make_async_copy(ref, dest, out_s.at[i])
+        for i, (ref, dest) in enumerate(zip(held, (qg_out, pg_out)))
+    ]
+    for take in takes:
+        take.start()
     gi_ref[...] = gi_in[...]
     part = inner_ref.shape[1] // 4
     for f in range(4):
-        wg_ref[:, f * part:(f + 1) * part] = lax.dot_general(
-            inp_ref[...], inner_ref[:, f * part:(f + 1) * part],
+        cut = pl.ds(f * part, part)
+        wg[:, cut] = lax.dot_general(
+            inp_ref[...], inner_ref[:, cut],
             (((0,), (0,)), ((), ())), preferred_element_type=jnp.float32,
-        ).astype(wg_ref.dtype)
-    for copy in copies:
-        copy.wait()
+        ).astype(wg.dtype)
+        gives.append(pltpu.make_async_copy(wg.at[:, cut], wg_out.at[:, cut], out_s.at[2 + f]))
+        gives[-1].start()
+    for take, give in zip(takes, gives):
+        take.wait()
+        give.start()
+    for give in gives:
+        give.wait()
 
 
 def plane_body(queries, passages, candidates, counts, teacher, section_weights, section_inputs, pre_acts):
@@ -658,8 +687,13 @@
             jax.ShapeDtypeStruct(section_weights.shape[1:], bf16),
         ),
         in_specs=[there, there, here, here, here],
-        out_specs=(there, there, here, here),
-        scratch_shapes=[dma((2,))],
+        out_specs=(there, there, here, there),
+        scratch_shapes=[
+            vmem(queries.shape, bf16),
+            vmem(passages.shape, bf16),
+            vmem(section_weights.shape[1:], bf16),
+            dma((2,)), dma((6,)),
+        ],
         compiler_params=pltpu.CompilerParams(vmem_limit_bytes=60 * 1024 * 1024),
     )(query_grads, passage_grads, grad_inputs, inner, section_inputs[0])
     return query_grads, passage_grads, grad_inputs[None], weight_grads[None]

time: 166 us -> 116 us (0.70)
  Pallas kernels: 165 us -> 115 us
    pallas_call x1, Pallas kernels: 58.8 us -> 4.54 us  [plane_body(): pl.pallas_call(finish_kernel, out_shape=(jax.ShapeDtypeStruct(queries.sha...]
    pallas_call x1, Pallas kernels: 106 us -> 110 us  [plane_body(): pl.pallas_call(relay_kernel, out_shape=(jax.ShapeDtypeStruct(queries.shap...]
where the time goes in v4:
time: 116 us
  Pallas kernels  115 us (99%)
    pallas_call x1, Pallas kernels, plane_body(): pl.pallas_call(relay_kernel, out_shape=(jax.ShapeDtypeStruct(queries.shap...  110 us
    pallas_call x1, Pallas kernels, plane_body(): pl.pallas_call(finish_kernel, out_shape=(jax.ShapeDtypeStruct(queries.sha...  4.54 us

profile of v4, /device:TPU:13, one launch (start us, length us, event | category | flops | bytes accessed | tf_op | source)
XLA Modules:
  0.0 115.6 jit_solution(16990406804132607072)
XLA Ops:
  0.6 110.2 %shard_map.111 = (bf16[128,3584]{1,0:T(8,128)(2,1)}, bf16[8,16,3584]{2,1,0:T(8,128)(2,1)}, f32[16,224]{1,0:T(8,128)}, bf16[16,3584]{1,0:T(8,128)(2,1)}) custom-call(bf16[128,3584]{1,0:T(8,128)(2,1)} %q_hbm.1, bf16[8,16,3584]{2,1,0:T(8,128)(2,1)} %p_ref.1, s32[3,16]{1,0:T(4,128)} %bitcast.10, s32[1,16]{1,0:T(1,128)} %bitcast.11, f32[128,384]{1,0:T(8,128)} %teacher_hbm.1, ...), custom_call_target="tpu_custom_call" | custom-call | tf_op jit(solution)/shard_map/pallas_call | solution.py:666
  110.9 4.5 %shard_map.112 = (bf16[128,3584]{1,0:T(8,128)(2,1)}, bf16[8,16,3584]{2,1,0:T(8,128)(2,1)}, f32[16,224]{1,0:T(8,128)}, bf16[224,3584]{1,0:T(8,128)(2,1)}) custom-call(bf16[128,3584]{1,0:T(8,128)(2,1)} %get-tuple-element.12.qg_in, bf16[8,16,3584]{2,1,0:T(8,128)(2,1)} %get-tuple-element.13.pg_in, f32[16,224]{1,0:T(8,128)} %get-tuple-element.14.gi_in, ...), custom_call_target="tpu_custom_call" | custom-call | tf_op jit(solution)/shard_map/pallas_call | solution.py:681

commit v5 on v4

--- a/solution.py
+++ b/solution.py
@@ -126,8 +126,7 @@
     return [(128 * a, 128 * (b - a)) for a, b in zip(edges, edges[1:])]
 
 
-CHUNKS = 3
-AHEAD = 3
+CHUNKS = 2
 
 
 def cells(width, ref, index):
@@ -138,8 +137,8 @@
     q_hbm, p_ref, cand_ref, count_ref, teacher_hbm, w_hbm, pre_ref,
     qg_hbm, pg_ref, gi_ref, inner_ref,
     q_ref, teacher_ref, w_ref, qg_ref, slope_ref, load_s, store_s,
-    candx, shard, up_in, down_in, sel, sel_t, stage, cols, target, terms, tin,
-    up_out, up_sum, down_out, down_sum, fin, final_in, prebuf, topbuf, cbuf, cot,
+    candx, line_in, sel, sel_t, stage, cols, target, terms, tin,
+    sum_out, sum_in, fin, final_in, prebuf, topbuf, cbuf, cot,
     cand_s, cand_r, half_s, half_r, line_s, line_r, pull_s, pull_r, push_s, push_r,
     sum_s, sum_r, fin_s, fin_r, pre_s, pre_r, top_s, top_r, cot_s, cot_r,
 ):
@@ -160,6 +159,9 @@
     micro, col = pre_ref.shape
     f32, bf16 = jnp.float32, jnp.bfloat16
     chunks = chunks_of(part, CHUNKS)
+    hops = z_count - 1
+    own_slot = 2 * hops
+    shard = line_in.at[own_slot]
 
     def lanes(c):
         return pl.ds(*chunks[c])
@@ -234,21 +236,23 @@
     )
     half_wait.wait_recv()
 
-    def line_copy(source, ref, sems, h, c, step):
+    def line_copy(source, d, h, c):
         return remote(
-            source.at[:, :, lanes(c)], ref.at[h, :, :, lanes(c)],
-            line_s.at[sems, h, c], line_r.at[sems, h, c], (section, dp + step * GROUP),
-        )
-
-    @pl.when(z < z_count - 1)
-    def _():
-        for c in range(CHUNKS):
-            line_copy(shard, up_in, 0, 0, c, 1).start()
-
-    @pl.when(z > 0)
-    def _():
-        for c in range(CHUNKS):
-            line_copy(shard, down_in, 1, 0, c, -1).start()
+            line_in.at[source, :, :, lanes(c)], line_in.at[d * hops + h, :, :, lanes(c)],
+            line_s.at[d, h, c], line_r.at[d, h, c], (section, dp + (1 - 2 * d) * GROUP),
+        )
+
+    def line_wait(d, h, c):
+        return remote(
+            line_in.at[own_slot, :, :, lanes(c)], line_in.at[d * hops + h, :, :, lanes(c)],
+            line_s.at[d, h, c], line_r.at[d, h, c], (section, dp - (1 - 2 * d) * GROUP),
+        )
+
+    for d, further in enumerate((z < z_count - 1, z > 0)):
+        @pl.when(further)
+        def _():
+            for c in range(CHUNKS):
+                line_copy(own_slot, d, 0, c).start()
 
     cand_copy.wait_recv()
     total = PLANE * slots * rows
@@ -279,19 +283,13 @@
     def pull_copy(zs, g, c):
         return remote(
             stage.at[zs, g, :, :, lanes(c)], cols.at[quarter, :, own_rows(zs, x), lanes(c)],
-            pull_s.at[zs, g, c], pull_r.at[zs, me, c], member(g),
-        )
-
-    def pull_wait(zs, g, c):
-        return remote(
-            stage.at[zs, g, :, :, lanes(c)], cols.at[g % 4, :, own_rows(zs, g // 4), lanes(c)],
-            pull_s.at[zs, g, c], pull_r.at[zs, g, c], member(g),
-        )
-
-    def spread(ref, zs, c):
+            pull_s.at[0], pull_r.at[c], member(g),
+        )
+
+    def spread(slot, zs, c):
         size = chunks[c][1]
         picked = jnp.dot(
-            sel[...], ref[:, :, lanes(c)].reshape(rows * block_total, size),
+            sel[...], line_in[slot, :, :, lanes(c)].reshape(rows * block_total, size),
             preferred_element_type=f32,
         )
         stage[zs, :, :, :, lanes(c)] = picked.astype(bf16).reshape(PLANE, slots, rows, size)
@@ -299,12 +297,12 @@
         cols[quarter, :, own_rows(zs, x), lanes(c)] = stage[zs, me, :, :, lanes(c)]
 
     for c in range(CHUNKS):
-        spread(shard, z, c)
+        spread(own_slot, z, c)
 
     prebuf[dp, :, :col] = pre_ref[...]
 
     def pre_copy(j):
-        return remote(prebuf.at[dp], prebuf.at[dp], pre_s.at[j], pre_r.at[dp], (section, j))
+        return remote(prebuf.at[dp], prebuf.at[dp], pre_s.at[0], pre_r.at[0], (section, j))
 
     others(dp_count, dp, lambda j: pre_copy(j).start())
 
@@ -323,68 +321,65 @@
     target[...] = soft(teacher_ref[...], valid)
     loads[0].wait()
 
+    beside = (section, dp + 1 - 2 * core)
+
+    def all_but_one(ref, send, recv):
+        return remote(ref, ref, send, recv, beside)
+
     def slopes():
-        others(dp_count, dp, lambda j: remote(
-            prebuf.at[j], prebuf.at[j], pre_s.at[j], pre_r.at[j], (section, j)).wait_recv())
+        all_but_one(prebuf.at[pl.ds(0, dp_count - 1)], pre_s.at[0], pre_r.at[0]).wait_recv()
         pre = jnp.concatenate([prebuf[j].astype(f32)[:, :col] for j in range(dp_count)], axis=1)
         sigma = 1.0 / (1.0 + jnp.exp(-pre))
         slope_ref[...] = sigma * (1.0 + pre * (1.0 - sigma))
 
-    def hop(h, c):
-        @pl.when(z >= h + 1)
-        def _():
-            line_copy(shard, up_in, 0, h, c, -1).wait_recv()
-            if h + 1 < z_count - 1:
-                @pl.when(z < z_count - 1)
+    def hop(h):
+        pl.when(h == hops - 1)(slopes)
+        for c in range(CHUNKS):
+            for d, came, further in ((0, z >= h + 1, z < z_count - 1), (1, z + h + 1 < z_count, z > 0)):
+                @pl.when(came)
                 def _():
-                    line_copy(up_in.at[h], up_in, 0, h + 1, c, 1).start()
-
-        @pl.when(z + h + 1 < z_count)
-        def _():
-            line_copy(shard, down_in, 1, h, c, 1).wait_recv()
-            if h + 1 < z_count - 1:
-                @pl.when(z > 0)
+                    line_wait(d, h, c).wait_recv()
+
+                    @pl.when(further & (h + 1 < hops))
+                    def _():
+                        line_copy(d * hops + h, d, h + 1, c).start()
+
+            def both(d):
+                zs = z - (1 - 2 * d) * (h + 1)
+
+                @pl.when((zs >= 0) & (zs < z_count))
                 def _():
-                    line_copy(down_in.at[h], down_in, 1, h + 1, c, -1).start()
-
-        @pl.when(z >= h + 1)
-        def _():
-            spread(up_in.at[h], z - h - 1, c)
-
-        @pl.when(z + h + 1 < z_count)
-        def _():
-            spread(down_in.at[h], z + h + 1, c)
-
-    for h in range(z_count - 1):
-        if h == z_count - 2:
-            slopes()
-        for c in range(CHUNKS):
-            hop(h, c)
+                    spread(d * hops + h, zs, c)
+
+            each(2, both)
+
+    each(hops, hop)
 
     contract_last = (((1,), (1,)), ((), ()))
     logits = jnp.zeros((block, slots * block), f32)
+
+    def lane_cut(f, c):
+        return pl.ds(pl.multiple_of(f * part + chunks[c][0], 128), chunks[c][1])
+
     for c, (offset, size) in enumerate(chunks):
-        for zs in range(z_count):
-            peers(lambda g: pull_wait(zs, g, c).wait_recv())
-        for f in range(4):
-            logits += lax.dot_general(
-                q_ref[:, f * part + offset:f * part + offset + size],
-                cols[f, :, :, lanes(c)].reshape(slots * block, size),
+        all_but_one(
+            stage.at[:, pl.ds(0, PLANE - 1), :, :, lanes(c)], pull_s.at[0], pull_r.at[c]
+        ).wait_recv()
+
+        def quarter_logits(f, carry):
+            return carry + lax.dot_general(
+                q_ref[:, lane_cut(f, c)], cols[f, :, :, lanes(c)].reshape(slots * block, size),
                 contract_last, preferred_element_type=f32,
             )
+
+        logits = lax.fori_loop(0, 4, quarter_logits, logits)
     weights32 = soft(logits * INVERSE_TEMP, valid) - target[...]
     weights = weights32.astype(bf16)
     weights_t = jnp.transpose(weights32).astype(bf16)
     def push_copy(zt, g, c):
         return remote(
             terms.at[g % 4, :, own_rows(zt, g // 4), lanes(c)], tin.at[zt, me, :, :, lanes(c)],
-            push_s.at[zt, g, c], push_r.at[zt, me, c], member(g),
-        )
-
-    def push_wait(zt, g, c):
-        return remote(
-            terms.at[quarter, :, own_rows(zt, x), lanes(c)], tin.at[zt, g, :, :, lanes(c)],
-            push_s.at[zt, g, c], push_r.at[zt, g, c], member(g),
+            push_s.at[0], push_r.at[zt, c], member(g),
         )
 
     def push(zt, c):
@@ -395,39 +390,43 @@
     orders = [sorted(range(z_count), key=lambda t: (-abs(t - own), -abs(2 * t - z_count + 1))) for own in range(z_count)]
 
     def target_at(i):
-        code = sum(orders[own][i] << (bits * own) for own in range(z_count))
-        return lax.shift_right_logical(jnp.int32(code), (bits * z).astype(jnp.int32)) % (1 << bits)
-
-    turns = [(i, c) for i in range(z_count) for c in range(CHUNKS)]
+        code = sum(
+            ((orders[own][at] - own) % z_count) << (bits * (at * z_count + own))
+            for at in range(z_count - 1) for own in range(z_count)
+        )
+        moved = lax.shift_right_logical(jnp.int32(code), (bits * (i * z_count + z)).astype(jnp.int32))
+        return (z + moved % (1 << bits)) % z_count
+
     for c, (offset, size) in enumerate(chunks):
-        for f in range(4):
-            sums = jnp.dot(
-                weights_t, q_ref[:, f * part + offset:f * part + offset + size],
-                preferred_element_type=f32,
-            )
+        def quarter_terms(f):
+            sums = jnp.dot(weights_t, q_ref[:, lane_cut(f, c)], preferred_element_type=f32)
             terms[f, :, :, lanes(c)] = (
                 (sums * INVERSE_TEMP).astype(bf16).reshape(slots, block, size)
             )
-        if c < AHEAD:
-            push(target_at(0), c)
-    for f in range(4):
+
+        each(4, quarter_terms)
+        push(target_at(z * 0), c)
+
+    def quarter_sums(f):
         sums = jnp.dot(weights, cols[f].reshape(slots * block, part), preferred_element_type=f32)
         sums = sums * INVERSE_TEMP
-        qg_ref[:, f * part:(f + 1) * part] = sums.astype(bf16)
-        topbuf[dp, :, f * part:(f + 1) * part] = sums[0:1]
-
+        span = pl.ds(pl.multiple_of(f * part, 128), part)
+        qg_ref[:, span] = sums.astype(bf16)
+        topbuf[dp, :, span] = sums[0:1]
+
+    each(4, quarter_sums)
     qg_copy = pltpu.make_async_copy(qg_ref, qg_hbm, store_s.at[0])
     qg_copy.start()
 
     def top_copy(j):
-        return remote(topbuf.at[dp], topbuf.at[dp], top_s.at[j], top_r.at[dp], (section, j))
+        return remote(topbuf.at[dp], topbuf.at[dp], top_s.at[0], top_r.at[0], (section, j))
 
     @pl.when(section == 1)
     def _():
         others(dp_count, dp, lambda j: top_copy(j).start())
 
     def cot_copy(j):
-        return remote(cbuf.at[dp], cbuf.at[dp], cot_s.at[j], cot_r.at[dp], (1 - section, j))
+        return remote(cbuf.at[dp], cbuf.at[dp], cot_s.at[0], cot_r.at[0], (1 - section, j))
 
     def layer(own):
         inner = (cot[...] * slope_ref[...]).astype(bf16)
@@ -439,8 +438,7 @@
         return updated
 
     def last_section():
-        others(dp_count, dp, lambda j: remote(
-            topbuf.at[j], topbuf.at[j], top_s.at[j], top_r.at[j], (section, j)).wait_recv())
+        all_but_one(topbuf.at[pl.ds(0, dp_count - 1)], top_s.at[0], top_r.at[0]).wait_recv()
         own = jnp.zeros((micro, col), f32)
         for j in range(dp_count):
             cot[j:j + 1, :] = topbuf[j]
@@ -451,41 +449,26 @@
         each(dp_count, lambda j: cot_copy(j).start())
 
     def summed(zt, c):
-        peers(lambda g: push_wait(zt, g, c).wait_recv())
+        all_but_one(
+            tin.at[zt, pl.ds(0, PLANE - 1), :, :, lanes(c)], push_s.at[0], push_r.at[zt, c]
+        ).wait_recv()
         size = chunks[c][1]
         return jnp.dot(
             sel_t[...], tin[zt, :, :, :, lanes(c)].reshape(total, size),
             preferred_element_type=f32,
         ).reshape(rows, block_total, size)
 
-    def sum_copy(source, dest, sems, h, c, step):
+    def sum_copy(d, h, c, step):
         return remote(
-            source.at[h, :, :, lanes(c)], dest.at[h, :, :, lanes(c)],
-            sum_s.at[sems, h, c], sum_r.at[sems, h, c], (section, dp + step * GROUP),
-        )
-
-    def line_sum(value, h, c, step, sems, out, incoming, beyond):
-        out[h - 1, :, :, lanes(c)] = value.astype(bf16)
-
-        @pl.when(beyond)
-        def _():
-            sum_copy(out, incoming, sems, h, c, -step).wait_recv()
-            both = value + incoming[h, :, :, lanes(c)].astype(f32)
-            out[h - 1, :, :, lanes(c)] = both.astype(bf16)
-
-        sum_copy(out, incoming, sems, h - 1, c, step).start()
+            sum_out.at[d, h, :, :, lanes(c)], sum_in.at[d, h, :, :, lanes(c)],
+            sum_s.at[d, h, c], sum_r.at[d, h, c], (section, dp + step * GROUP),
+        )
 
     def fin_copy(i, c):
         return remote(
             fin.at[pl.ds((i % 2) * stripe, stripe), :, lanes(c)],
             final_in.at[quarter, :, :, lanes(c)],
-            fin_s.at[i, c], fin_r.at[quarter, c], (i // 2, z * GROUP + x * 2 + i % 2),
-        )
-
-    def fin_wait(i, c):
-        return remote(
-            fin.at[pl.ds(core * stripe, stripe), :, lanes(c)], final_in.at[i, :, :, lanes(c)],
-            fin_s.at[i, c], fin_r.at[i, c], (i // 2, z * GROUP + x * 2 + i % 2),
+            fin_s.at[0], fin_r.at[c], (i // 2, z * GROUP + x * 2 + i % 2),
         )
 
     def own_sum(value, c):
@@ -493,89 +476,83 @@
 
         @pl.when(z > 0)
         def _():
-            sum_copy(up_out, up_sum, 0, 0, c, -1).wait_recv()
+            sum_copy(0, 0, c, -1).wait_recv()
 
         @pl.when(z < z_count - 1)
         def _():
-            sum_copy(down_out, down_sum, 1, 0, c, 1).wait_recv()
-
-        below = jnp.where(z > 0, up_sum[0, :, :, lanes(c)].astype(f32), zero)
-        above = jnp.where(z < z_count - 1, down_sum[0, :, :, lanes(c)].astype(f32), zero)
+            sum_copy(1, 0, c, 1).wait_recv()
+
+        below = jnp.where(z > 0, sum_in[0, 0, :, :, lanes(c)].astype(f32), zero)
+        above = jnp.where(z < z_count - 1, sum_in[1, 0, :, :, lanes(c)].astype(f32), zero)
         fin[:, :, lanes(c)] = (value + below + above).astype(bf16)
         others(4, quarter, lambda i: fin_copy(i, c).start())
         final_in[quarter, :, :, lanes(c)] = fin[pl.ds(core * stripe, stripe), :, lanes(c)]
 
-    for turn, (i, c) in enumerate(turns):
+    def turn(i):
         zt = target_at(i)
-        value = summed(zt, c)
-        if turn + AHEAD < len(turns):
-            push(target_at(turns[turn + AHEAD][0]), turns[turn + AHEAD][1])
-        if i == z_count - 1:
-            own_sum(value, c)
-            continue
-
-        @pl.when(zt > z)
-        def _():
-            line_sum(value, zt - z, c, 1, 0, up_out, up_sum, z > 0)
-
-        @pl.when(zt < z)
-        def _():
-            line_sum(value, z - zt, c, -1, 1, down_out, down_sum, z < z_count - 1)
-
-        if turn == CHUNKS:
-            pl.when(section == 1)(last_section)
+        d = 1 - (zt - z - 1 + z_count) // z_count
+        step = 1 - 2 * d
+        h = (zt - z) * step
+        for c in range(CHUNKS):
+            value = summed(zt, c)
+            push(target_at(i + 1), c)
+            sum_out[d, h - 1, :, :, lanes(c)] = value.astype(bf16)
+
+            @pl.when(z != d * (z_count - 1))
+            def _():
+                sum_copy(d, h, c, -step).wait_recv()
+                both = value + sum_in[d, h, :, :, lanes(c)].astype(f32)
+                sum_out[d, h - 1, :, :, lanes(c)] = both.astype(bf16)
+
+            sum_copy(d, h - 1, c, step).start()
+
+        pl.when((section == 1) & (i == 0))(last_section)
+
+    each(z_count - 1, turn)
+    for c in range(CHUNKS):
+        own_sum(summed(z, c), c)
 
     @pl.when(section == 0)
     def _():
-        def wait(j, carry):
-            remote(cbuf.at[j], cbuf.at[j], cot_s.at[j], cot_r.at[j], (1 - section, j)).wait_recv()
-            return carry
-        lax.fori_loop(0, dp_count, wait, 0)
+        remote(cbuf, cbuf, cot_s.at[0], cot_r.at[0], (1 - section, dp)).wait_recv()
         cot[...] = jnp.concatenate([cbuf[j][:, :col] for j in range(dp_count)], axis=1)
         layer(cbuf[dp][:, :col])
-
-    for c in range(CHUNKS):
-        others(4, quarter, lambda i: fin_wait(i, c).wait_recv())
-    for f in range(4):
-        pg_ref[:, :, f * part:(f + 1) * part] = final_in[f]
 
     qg_copy.wait()
     cand_copy.wait_send()
     half_copy.wait_send()
-    for h in range(z_count - 1):
+
+    def line_sent(h):
         for c in range(CHUNKS):
-            @pl.when((z >= h) & (z < z_count - 1))
-            def _():
-                line_copy(up_in.at[h], up_in, 0, h, c, 1).wait_send()
-
-            @pl.when((z + h < z_count) & (z > 0))
-            def _():
-                line_copy(down_in.at[h], down_in, 1, h, c, -1).wait_send()
-
-            @pl.when(z + h + 1 < z_count)
-            def _():
-                sum_copy(up_out, up_sum, 0, h, c, 1).wait_send()
-
-            @pl.when(z >= h + 1)
-            def _():
-                sum_copy(down_out, down_sum, 1, h, c, -1).wait_send()
-
-    def sent(zs, carry):
-        for c in range(CHUNKS):
-            peers(lambda g: pull_copy(zs, g, c).wait_send())
-            peers(lambda g: push_copy(zs, g, c).wait_send())
-        return carry
-
-    lax.fori_loop(0, z_count, sent, 0)
-    others(dp_count, dp, lambda j: pre_copy(j).wait_send())
+            for d, begun, further in ((0, z >= h, z < z_count - 1), (1, z + h < z_count, z > 0)):
+                @pl.when(begun & further)
+                def _():
+                    line_copy(own_slot, d, h, c).wait_send()
+
+            for d, held in ((0, z + h + 1 < z_count), (1, z >= h + 1)):
+                @pl.when(held)
+                def _():
+                    sum_copy(d, h, c, 1 - 2 * d).wait_send()
+
+    each(hops, line_sent)
+    seven = pl.ds(0, PLANE - 1)
+    all_but_one(stage.at[:, seven], pull_s.at[0], pull_r.at[0]).wait_send()
+    all_but_one(tin.at[:, seven], push_s.at[0], pull_r.at[0]).wait_send()
+    fifteen = pl.ds(0, dp_count - 1)
+    all_but_one(prebuf.at[fifteen], pre_s.at[0], pre_r.at[0]).wait_send()
 
     @pl.when(section == 1)
     def _():
-        others(dp_count, dp, lambda j: top_copy(j).wait_send())
-        each(dp_count, lambda j: cot_copy(j).wait_send())
+        all_but_one(topbuf.at[fifteen], top_s.at[0], top_r.at[0]).wait_send()
+        all_but_one(cbuf, cot_s.at[0], cot_r.at[0]).wait_send()
 
     for c in range(CHUNKS):
-        others(4, quarter, lambda i: fin_copy(i, c).wait_send())
+        all_but_one(
+            final_in.at[pl.ds(0, 3), :, :, lanes(c)], fin_s.at[0], fin_r.at[c]
+        ).wait_recv()
+    for f in range(4):
+        pg_ref[:, :, f * part:(f + 1) * part] = final_in[f]
+    all_but_one(final_in.at[pl.ds(0, 3)], fin_s.at[0], fin_r.at[0]).wait_send()
 
 
 def finish_kernel(
@@ -632,9 +609,7 @@
         vmem((micro, width), f32),
         dma((3,)), dma((1,)),
         vmem(table.shape, i32),
-        vmem((rows, block_total, part), bf16),
-        vmem((hop, rows, block_total, part), bf16),
-        vmem((hop, rows, block_total, part), bf16),
+        vmem((2 * hop + 1, rows, block_total, part), bf16),
         vmem((PLANE * slots * rows, rows * block_total), bf16),
         vmem((rows * block_total, PLANE * slots * rows), bf16),
         vmem((z_count, PLANE, slots, rows, part), bf16),
@@ -642,10 +617,8 @@
         vmem((block, slots * block), f32),
         vmem((4, slots, block, part), bf16),
         vmem((z_count, PLANE, slots, rows, part), bf16),
-        vmem((hop, rows, block_total, part), bf16),
-        vmem((hop, rows, block_total, part), bf16),
-        vmem((hop, rows, block_total, part), bf16),
-        vmem((hop, rows, block_total, part), bf16),
+        vmem((2, hop, rows, block_total, part), bf16),
+        vmem((2, hop, rows, block_total, part), bf16),
         vmem((rows, block_total, part), bf16),
         vmem((4, stripe, block_total, part), bf16),
         vmem((dp_count, micro, wide), bf16),
@@ -654,13 +627,13 @@
         vmem((micro, width), f32),
         dma((1,)), dma((1,)), dma((1,)), dma((1,)),
         dma((2, hop, CHUNKS)), dma((2, hop, CHUNKS)),
-        dma((z_count, PLANE, CHUNKS)), dma((z_count, PLANE, CHUNKS)),
-        dma((z_count, PLANE, CHUNKS)), dma((z_count, PLANE, CHUNKS)),
+        dma((1,)), dma((CHUNKS,)),
+        dma((1,)), dma((z_count, CHUNKS)),
         dma((2, hop, CHUNKS)), dma((2, hop, CHUNKS)),
-        dma((4, CHUNKS)), dma((4, CHUNKS)),
-        dma((dp_count,)), dma((dp_count,)),
-        dma((dp_count,)), dma((dp_count,)),
-        dma((dp_count,)), dma((dp_count,)),
+        dma((1,)), dma((CHUNKS,)),
+        dma((1,)), dma((1,)),
+        dma((1,)), dma((1,)),
+        dma((1,)), dma((1,)),
     ]
     here, there = pl.BlockSpec(memory_space=vmem), pl.BlockSpec(memory_space=pl.ANY)
     query_grads, passage_grads, grad_inputs, inner = pl.pallas_call(

time: 116 us -> 106 us (0.914)
  Pallas kernels: 115 us -> 105 us
    pallas_call x1, Pallas kernels: 110 us -> 101 us  [plane_body(): pl.pallas_call(relay_kernel, out_shape=(jax.ShapeDtypeStruct(queries.shap...]
where the time goes in v5:
time: 106 us
  Pallas kernels  105 us (99%)
    pallas_call x1, Pallas kernels, plane_body(): pl.pallas_call(relay_kernel, out_shape=(jax.ShapeDtypeStruct(queries.shap...  101 us
    pallas_call x1, Pallas kernels, plane_body(): pl.pallas_call(finish_kernel, out_shape=(jax.ShapeDtypeStruct(queries.sha...  4.54 us

profile of v5, /device:TPU:13, one launch (start us, length us, event | category | flops | bytes accessed | tf_op | source)
XLA Modules:
  0.0 106.0 jit_solution(3310416950991375386)
XLA Ops:
  0.6 100.8 %shard_map.111 = (bf16[128,3584]{1,0:T(8,128)(2,1)}, bf16[8,16,3584]{2,1,0:T(8,128)(2,1)}, f32[16,224]{1,0:T(8,128)}, bf16[16,3584]{1,0:T(8,128)(2,1)}) custom-call(bf16[128,3584]{1,0:T(8,128)(2,1)} %q_hbm.1, bf16[8,16,3584]{2,1,0:T(8,128)(2,1)} %p_ref.1, s32[3,16]{1,0:T(4,128)} %bitcast.10, s32[1,16]{1,0:T(1,128)} %bitcast.11, f32[128,384]{1,0:T(8,128)} %teacher_hbm.1, ...), custom_call_target="tpu_custom_call" | custom-call | tf_op jit(solution)/shard_map/pallas_call | solution.py:639
  101.5 4.5 %shard_map.112 = (bf16[128,3584]{1,0:T(8,128)(2,1)}, bf16[8,16,3584]{2,1,0:T(8,128)(2,1)}, f32[16,224]{1,0:T(8,128)}, bf16[224,3584]{1,0:T(8,128)(2,1)}) custom-call(bf16[128,3584]{1,0:T(8,128)(2,1)} %get-tuple-element.12.qg_in, bf16[8,16,3584]{2,1,0:T(8,128)(2,1)} %get-tuple-element.13.pg_in, f32[16,224]{1,0:T(8,128)} %get-tuple-element.14.gi_in, ...), custom_call_target="tpu_custom_call" | custom-call | tf_op jit(solution)/shard_map/pallas_call | solution.py:654

commit v6 on v5

--- a/solution.py
+++ b/solution.py
@@ -126,7 +126,7 @@
     return [(128 * a, 128 * (b - a)) for a, b in zip(edges, edges[1:])]
 
 
-CHUNKS = 2
+CHUNKS = 3
 
 
 def cells(width, ref, index):
@@ -134,9 +134,9 @@
 
 
 def relay_kernel(
-    q_hbm, p_ref, cand_ref, count_ref, teacher_hbm, w_hbm, pre_ref,
-    qg_hbm, pg_ref, gi_ref, inner_ref,
-    q_ref, teacher_ref, w_ref, qg_ref, slope_ref, load_s, store_s,
+    q_hbm, p_hbm, cand_ref, count_ref, teacher_hbm, w_hbm, pre_ref,
+    qg_hbm, pg_hbm, gi_ref, inner_ref,
+    p_ref, q_ref, teacher_ref, w_ref, qg_ref, slope_ref, load_s, store_s,
     candx, line_in, sel, sel_t, stage, cols, target, terms, tin,
     sum_out, sum_in, fin, final_in, prebuf, topbuf, cbuf, cot,
     cand_s, cand_r, half_s, half_r, line_s, line_r, pull_s, pull_r, push_s, push_r,
@@ -204,7 +204,14 @@
             ((q_hbm, q_ref), (teacher_hbm, teacher_ref), (w_hbm, w_ref))
         )
     ]
-    for load in loads:
+    rows_in = [
+        pltpu.make_async_copy(
+            p_hbm.at[:, :, pl.ds(f * part, part)], p_ref.at[:, :, pl.ds(f * part, part)],
+            load_s.at[len(loads) + f],
+        )
+        for f in range(4)
+    ]
+    for load in rows_in + loads:
         load.start()
 
     barrier = pltpu.get_barrier_semaphore()
@@ -222,6 +229,8 @@
     cand_copy = remote(cand_ref, candx, cand_s.at[0], cand_r.at[0], (1 - section, dp))
     cand_copy.start()
     partner = dp + 1 - 2 * core
+    for load in rows_in:
+        load.wait()
     half_copy = remote(
         cells(part, p_ref, section * 2 + 1 - core), shard.at[pl.ds(core * stripe, stripe)],
         half_s.at[0], half_r.at[0], (section, partner),
@@ -546,12 +555,20 @@
         all_but_one(topbuf.at[fifteen], top_s.at[0], top_r.at[0]).wait_send()
         all_but_one(cbuf, cot_s.at[0], cot_r.at[0]).wait_send()
 
+    rows_out = []
     for c in range(CHUNKS):
         all_but_one(
             final_in.at[pl.ds(0, 3), :, :, lanes(c)], fin_s.at[0], fin_r.at[c]
         ).wait_recv()
-    for f in range(4):
-        pg_ref[:, :, f * part:(f + 1) * part] = final_in[f]
+        for f in range(4):
+            rows_out.append(pltpu.make_async_copy(
+                final_in.at[f, :, :, lanes(c)],
+                pg_hbm.at[:, :, pl.ds(f * part + chunks[c][0], chunks[c][1])],
+                store_s.at[1 + c * 4 + f],
+            ))
+            rows_out[-1].start()
+    for copy in rows_out:
+        copy.wait()
     all_but_one(final_in.at[pl.ds(0, 3)], fin_s.at[0], fin_r.at[0]).wait_send()
 
 
@@ -559,31 +576,30 @@
     qg_in, pg_in, gi_in, inner_ref, inp_ref, qg_out, pg_out, gi_ref, wg_out,
     qg, pg, wg, in_s, out_s,
 ):
-    held = (qg, pg)
-    takes = [
-        pltpu.make_async_copy(source, ref, in_s.at[i])
-        for i, (source, ref) in enumerate(zip((qg_in, pg_in), held))
-    ]
-    gives = [
-        pltpu.make_async_copy(ref, dest, out_s.at[i])
-        for i, (ref, dest) in enumerate(zip(held, (qg_out, pg_out)))
-    ]
+    part = inner_ref.shape[1] // 4
+    takes, gives = [], []
+    for f in range(4):
+        cut = pl.ds(f * part, part)
+        for i, (source, ref, dest) in enumerate(((qg_in, qg, qg_out), (pg_in, pg, pg_out))):
+            at = (slice(None),) * (len(ref.shape) - 1) + (cut,)
+            takes.append(pltpu.make_async_copy(source.at[at], ref.at[at], in_s.at[2 * f + i]))
+            gives.append(pltpu.make_async_copy(ref.at[at], dest.at[at], out_s.at[4 + 2 * f + i]))
     for take in takes:
         take.start()
     gi_ref[...] = gi_in[...]
-    part = inner_ref.shape[1] // 4
+    outer = []
     for f in range(4):
         cut = pl.ds(f * part, part)
         wg[:, cut] = lax.dot_general(
             inp_ref[...], inner_ref[:, cut],
             (((0,), (0,)), ((), ())), preferred_element_type=jnp.float32,
         ).astype(wg.dtype)
-        gives.append(pltpu.make_async_copy(wg.at[:, cut], wg_out.at[:, cut], out_s.at[2 + f]))
-        gives[-1].start()
+        outer.append(pltpu.make_async_copy(wg.at[:, cut], wg_out.at[:, cut], out_s.at[f]))
+        outer[-1].start()
     for take, give in zip(takes, gives):
         take.wait()
         give.start()
-    for give in gives:
+    for give in gives + outer:
         give.wait()
 
 
@@ -602,12 +618,13 @@
     vmem, dma = pltpu.VMEM, pltpu.SemaphoreType.DMA
     hop = z_count - 1
     scratch = [
+        vmem(passages.shape, bf16),
         vmem(queries.shape, bf16),
         vmem(teacher.shape, f32),
         vmem(section_weights.shape[1:], bf16),
         vmem(queries.shape, bf16),
         vmem((micro, width), f32),
-        dma((3,)), dma((1,)),
+        dma((7,)), dma((1 + 4 * CHUNKS,)),
         vmem(table.shape, i32),
         vmem((2 * hop + 1, rows, block_total, part), bf16),
         vmem((PLANE * slots * rows, rows * block_total), bf16),
@@ -644,8 +661,8 @@
             jax.ShapeDtypeStruct((micro, col), f32),
             jax.ShapeDtypeStruct((micro, width), bf16),
         ),
-        in_specs=[there, here, here, here, there, there, here],
-        out_specs=(there, here, here, here),
+        in_specs=[there, there, here, here, there, there, here],
+        out_specs=(there, there, here, here),
         scratch_shapes=scratch,
         compiler_params=pltpu.CompilerParams(
             collective_id=0, has_side_effects=True, vmem_limit_bytes=56 * 1024 * 1024
@@ -665,7 +682,7 @@
             vmem(queries.shape, bf16),
             vmem(passages.shape, bf16),
             vmem(section_weights.shape[1:], bf16),
-            dma((2,)), dma((6,)),
+            dma((8,)), dma((12,)),
         ],
         compiler_params=pltpu.CompilerParams(vmem_limit_bytes=60 * 1024 * 1024),
     )(query_grads, passage_grads, grad_inputs, inner, section_inputs[0])

time: 106 us -> 105 us (level)
  no operation moved by 1% of the time
where the time goes in v6:
time: 105 us
  Pallas kernels  105 us (100%)
    pallas_call x1, Pallas kernels, plane_body(): pl.pallas_call(relay_kernel, out_shape=(jax.ShapeDtypeStruct(queries.shap...  99.8 us
    pallas_call x1, Pallas kernels, plane_body(): pl.pallas_call(finish_kernel, out_shape=(jax.ShapeDtypeStruct(queries.sha...  4.83 us

profile of v6, /device:TPU:13, one launch (start us, length us, event | category | flops | bytes accessed | tf_op | source)
XLA Modules:
  0.0 105.3 jit_solution(17430087875107119616)
XLA Ops:
  0.6 99.8 %shard_map.111 = (bf16[128,3584]{1,0:T(8,128)(2,1)}, bf16[8,16,3584]{2,1,0:T(8,128)(2,1)}, f32[16,224]{1,0:T(8,128)}, bf16[16,3584]{1,0:T(8,128)(2,1)}) custom-call(bf16[128,3584]{1,0:T(8,128)(2,1)} %q_hbm.1, bf16[8,16,3584]{2,1,0:T(8,128)(2,1)} %p_hbm.1, s32[3,16]{1,0:T(4,128)} %bitcast.10, s32[1,16]{1,0:T(1,128)} %bitcast.11, f32[128,384]{1,0:T(8,128)} %teacher_hbm.1, ...), custom_call_target="tpu_custom_call" | custom-call | tf_op jit(solution)/shard_map/pallas_call | solution.py:656
  100.4 4.8 %shard_map.112 = (bf16[128,3584]{1,0:T(8,128)(2,1)}, bf16[8,16,3584]{2,1,0:T(8,128)(2,1)}, f32[16,224]{1,0:T(8,128)}, bf16[224,3584]{1,0:T(8,128)(2,1)}) custom-call(bf16[128,3584]{1,0:T(8,128)(2,1)} %get-tuple-element.12.qg_in, bf16[8,16,3584]{2,1,0:T(8,128)(2,1)} %get-tuple-element.13.pg_in, f32[16,224]{1,0:T(8,128)} %get-tuple-element.14.gi_in, ...), custom_call_target="tpu_custom_call" | custom-call | tf_op jit(solution)/shard_map/pallas_call | solution.py:671

commit v7 on v6

--- a/solution.py
+++ b/solution.py
@@ -126,7 +126,7 @@
     return [(128 * a, 128 * (b - a)) for a, b in zip(edges, edges[1:])]
 
 
-CHUNKS = 3
+CHUNKS = 2
 
 
 def cells(width, ref, index):

time: 105 us -> 106 us (level)
  no operation moved by 1% of the time
where the time goes in v7:
time: 106 us
  Pallas kernels  105 us (99%)
    pallas_call x1, Pallas kernels, plane_body(): pl.pallas_call(relay_kernel, out_shape=(jax.ShapeDtypeStruct(queries.shap...  100 us
    pallas_call x1, Pallas kernels, plane_body(): pl.pallas_call(finish_kernel, out_shape=(jax.ShapeDtypeStruct(queries.sha...  4.83 us

profile of v7, /device:TPU:13, one launch (start us, length us, event | category | flops | bytes accessed | tf_op | source)
XLA Modules:
  0.0 105.7 jit_solution(11763848004461880126)
XLA Ops:
  0.6 100.2 %shard_map.111 = (bf16[128,3584]{1,0:T(8,128)(2,1)}, bf16[8,16,3584]{2,1,0:T(8,128)(2,1)}, f32[16,224]{1,0:T(8,128)}, bf16[16,3584]{1,0:T(8,128)(2,1)}) custom-call(bf16[128,3584]{1,0:T(8,128)(2,1)} %q_hbm.1, bf16[8,16,3584]{2,1,0:T(8,128)(2,1)} %p_hbm.1, s32[3,16]{1,0:T(4,128)} %bitcast.10, s32[1,16]{1,0:T(1,128)} %bitcast.11, f32[128,384]{1,0:T(8,128)} %teacher_hbm.1, ...), custom_call_target="tpu_custom_call" | custom-call | tf_op jit(solution)/shard_map/pallas_call | solution.py:656
  100.8 4.8 %shard_map.112 = (bf16[128,3584]{1,0:T(8,128)(2,1)}, bf16[8,16,3584]{2,1,0:T(8,128)(2,1)}, f32[16,224]{1,0:T(8,128)}, bf16[224,3584]{1,0:T(8,128)(2,1)}) custom-call(bf16[128,3584]{1,0:T(8,128)(2,1)} %get-tuple-element.12.qg_in, bf16[8,16,3584]{2,1,0:T(8,128)(2,1)} %get-tuple-element.13.pg_in, f32[16,224]{1,0:T(8,128)} %get-tuple-element.14.gi_in, ...), custom_call_target="tpu_custom_call" | custom-call | tf_op jit(solution)/shard_map/pallas_call | solution.py:671
